TPU v7x, 32 devices: a whole 2x2x4 slice. The times are simulated.
32 devices in a mesh: fsdp: 4 (over z), seq: 8 (over y, x, core).
Axes of the slice: x: 2, y: 2, z: 4, core: 2. Of those that a mesh axis runs over, the one named last changes fastest.
Arguments:
- queries: bfloat16 [4, 2048, 2048], P('fsdp', 'seq'), may hold values from -32 to 32
- keys: bfloat16 [4, 2048, 2048], P('fsdp', 'seq'), may hold values from -6 to 6
- values: bfloat16 [4, 2048, 2048], P('fsdp', 'seq'), may hold values from -6 to 6
- out_grad: bfloat16 [4, 2048, 2048], P('fsdp', 'seq'), may hold values from -6 to 6
- out_weight: bfloat16 [2048, 2048], P('fsdp'), may hold values from -0.125 to 0.125
- key_blocks: int32 [4, 16, 10], P('fsdp'), may hold values from 0 to 15, as said below
- block_counts: int32 [4, 16], P('fsdp'), may hold values from 2 to 10, as said below
Outputs:
- query_grad: bfloat16 [4, 2048, 2048], P('fsdp', 'seq')
- key_grad: bfloat16 [4, 2048, 2048], P('fsdp', 'seq')
- value_grad: bfloat16 [4, 2048, 2048], P('fsdp', 'seq')
- wo_grad: float32 [2048, 2048], P('fsdp')
Inputs may be any that keep to these rules, and one draw needn't show every extreme that they name: `key_blocks`: within a row the numbers are distinct; slots 0, 1 and 2 hold blocks i, i + 1 and i - 1 modulo 16; slots at or past the row's count are ignored. `block_counts`: every sample has a query block whose count is 10.
All inputs are finite; a program needn't handle non-finite values.
Results may differ from a plain program's by a relative error of at most 0.025.
Values may be sent and summed in bfloat16 or wider, within the bound.
No kernel may reach another device: no remote copies, remote signals or barrier semaphores. Data moves between devices by JAX's collectives and lax.ppermute only.
A program may use at most 128 MiB of HBM per device.

v0:
```python
import functools
import math

import jax
import jax.numpy as jnp
from jax import lax
from jax.experimental import pallas as pl
from jax.experimental.pallas import tpu as pltpu
from jax.sharding import PartitionSpec as P

HEADS = 32
HD = 64
BLK = 128
MAXK = 10


NEG_FILL = -1e30


def pair_scores(query_blocks, chosen):
    return jnp.einsum(
        "iqhd,ikhd->ihqk", query_blocks, chosen, preferred_element_type=jnp.float32
    ) * HD ** (-0.5)


def blocked(array):
    return array.reshape(-1, BLK, array.shape[1], HD)


def head_forward(query_h, key_h, value_h, adjacency, slot_live):
    query_blocks = blocked(query_h)
    key_heads = blocked(key_h)
    value_heads = blocked(value_h)
    blocks_total = query_blocks.shape[0]
    head_count = query_blocks.shape[2]

    def stat_step(carried, slot):
        row_max, row_sum = carried
        score = pair_scores(query_blocks, key_heads[adjacency[:, slot]])
        usable = slot_live[:, slot][:, None, None, None]
        score = jnp.where(usable, score, NEG_FILL)
        new_max = jnp.maximum(row_max, jnp.max(score, axis=-1))
        expo = jnp.where(usable, jnp.exp(score - new_max[..., None]), 0.0)
        row_sum = row_sum * jnp.exp(row_max - new_max) + jnp.sum(expo, axis=-1)
        return ((new_max, row_sum), None)

    start_max = jnp.full((blocks_total, head_count, BLK), NEG_FILL, jnp.float32)
    start_sum = jnp.zeros((blocks_total, head_count, BLK), jnp.float32)
    (row_max, row_sum), _ = lax.scan(stat_step, (start_max, start_sum), jnp.arange(MAXK))

    def output_step(accum, slot):
        picked = adjacency[:, slot]
        score = pair_scores(query_blocks, key_heads[picked])
        usable = slot_live[:, slot][:, None, None, None]
        prob_half = jnp.where(
            usable, jnp.exp(score - row_max[..., None]) / row_sum[..., None], 0.0
        ).astype(jnp.bfloat16)
        accum = accum + jnp.einsum(
            "ihqk,ikhd->iqhd", prob_half, value_heads[picked], preferred_element_type=jnp.float32
        )
        return (accum, None)

    start_out = jnp.zeros(query_blocks.shape, jnp.float32)
    accum, _ = lax.scan(output_step, start_out, jnp.arange(MAXK))
    return (row_max, row_sum, accum.astype(jnp.bfloat16))


def head_backward(
    query_h, key_h, value_h, grad_h, row_max, row_sum, attn_blocks, adjacency, slot_live
):
    query_blocks = blocked(query_h)
    key_heads = blocked(key_h)
    value_heads = blocked(value_h)
    grad_blocks = blocked(grad_h)
    scale_factor = HD ** (-0.5)
    row_dot = jnp.sum(
        grad_blocks.astype(jnp.float32) * attn_blocks.astype(jnp.float32), axis=-1
    ).transpose(0, 2, 1)

    def grad_step(carried, slot):
        query_accum, key_accum, value_accum = carried
        picked = adjacency[:, slot]
        chosen_keys = key_heads[picked]
        chosen_values = value_heads[picked]
        score = pair_scores(query_blocks, chosen_keys)
        usable = slot_live[:, slot][:, None, None, None]
        prob_full = jnp.where(usable, jnp.exp(score - row_max[..., None]) / row_sum[..., None], 0.0)
        prob_half = prob_full.astype(jnp.bfloat16)
        prob_grad = jnp.einsum(
            "iqhd,ikhd->ihqk", grad_blocks, chosen_values, preferred_element_type=jnp.float32
        )
        score_grad = (prob_full * (prob_grad - row_dot[..., None])).astype(jnp.bfloat16)
        query_accum = (
            query_accum
            + jnp.einsum(
                "ihqk,ikhd->iqhd", score_grad, chosen_keys, preferred_element_type=jnp.float32
            )
            * scale_factor
        )
        key_terms = (
            jnp.einsum(
                "ihqk,iqhd->ikhd", score_grad, query_blocks, preferred_element_type=jnp.float32
            )
            * scale_factor
        )
        value_terms = jnp.einsum(
            "ihqk,iqhd->ikhd", prob_half, grad_blocks, preferred_element_type=jnp.float32
        )
        key_accum = key_accum.at[picked].add(key_terms)
        value_accum = value_accum.at[picked].add(value_terms)
        return ((query_accum, key_accum, value_accum), None)

    zeros_start = jnp.zeros(query_blocks.shape, jnp.float32)
    (query_accum, key_accum, value_accum), _ = lax.scan(
        grad_step, (zeros_start, zeros_start, zeros_start), jnp.arange(MAXK)
    )
    head_count = query_h.shape[1]
    return tuple(
        (
            accum.astype(jnp.bfloat16).reshape(-1, head_count, HD)
            for accum in (query_accum, key_accum, value_accum)
        )
    )


PAIR = 2 * HD
SCALE = HD ** (-0.5)
BASE2 = SCALE * math.log2(math.e)


def fold_rows(tile, combine):
    return combine(tile.reshape(-1, 8, tile.shape[1]), axis=0)


def block_rows(index, height=BLK):
    return pl.ds(pl.multiple_of(index * height, height), height)


def by_head(block):
    first = lax.broadcasted_iota(jnp.int32, block.shape, 1) < HD
    zero = jnp.zeros_like(block)
    return jnp.concatenate([jnp.where(first, block, zero), jnp.where(first, zero, block)], axis=0)


def by_head_t(block):
    turned = block.T
    first = lax.broadcasted_iota(jnp.int32, turned.shape, 0) < HD
    zero = jnp.zeros_like(turned)
    return jnp.concatenate([jnp.where(first, turned, zero), jnp.where(first, zero, turned)], axis=1)


def own_parts(wide):
    return jnp.concatenate([wide[:HD, :BLK], wide[HD:, BLK:]], axis=0)


def columns(pair, part):
    return pl.ds(PAIR * (3 * pair + part), PAIR)


def dot(left, right):
    return lax.dot_general(left, right, (((1,), (0,)), ((), ())), preferred_element_type=jnp.float32)


def stack(source, places, right):
    return dot(jnp.concatenate([source[at, :] for at in places], axis=0), right)


def each_block(counts, begin, end, step, body):
    @pl.loop(begin, end)
    def _(index):
        for slots in range(2, MAXK + 1, step):
            @pl.when((counts[index] + step - 1) // step * step == slots)
            def _():
                body(index, slots)


def forward_kernel(adjacency, counts, packed, *refs, begin, end):
    carried, (first, second, stats, value_t) = refs[:-4], refs[-4:]
    outs = (first, second)
    blocks = packed.shape[0] // BLK
    if begin:
        done = pl.ds(0, BLK * begin)
        first[done, :], second[done, :] = carried[0][done, :], carried[1][done, :]
        stats[:, : 8 * begin, :] = carried[2][:, : 8 * begin, :]

    @pl.loop(0, blocks)
    def _(index):
        for pair in range(2):
            value_t[pair, index] = packed[block_rows(index), columns(pair, 2)].T

    def query_block(index, slots):
        picked = [adjacency[index, slot] for slot in range(slots)]
        places = [block_rows(block) for block in picked]
        raws = []
        for pair in range(2):
            queries = by_head_t(packed[block_rows(index), columns(pair, 0)])
            raw = stack(packed.at[:, columns(pair, 1)], places, queries)
            unsure = jnp.where(slots - 1 < counts[index], raw[-BLK:], NEG_FILL)
            raws.append(jnp.concatenate([raw[:-BLK], unsure], axis=0))
        for pair, raw in enumerate(raws):
            row_max = jnp.max(fold_rows(raw, jnp.max), axis=0, keepdims=True)
            expo = jnp.exp2((raw - row_max) * BASE2)
            row_sum = jnp.sum(fold_rows(expo, jnp.sum), axis=0, keepdims=True)
            out_t = dot(
                jnp.concatenate([value_t[pair, block] for block in picked], axis=1),
                expo.astype(jnp.bfloat16),
            )
            outs[pair][block_rows(index), :] = own_parts(out_t / row_sum).T.astype(jnp.bfloat16)
            stats[pair, block_rows(index, 8), :] = jnp.broadcast_to(
                row_max * BASE2 + jnp.log2(row_sum), (8, 2 * BLK)
            )

    each_block(counts, begin, end, 2, query_block)


def backward_kernel(
    adjacency, counts, packed, grad, attn_out, stats, *refs, blocks, begin, end
):
    query, key, value = (packed.at[:, pl.ds(PAIR * part, PAIR)] for part in range(3))
    carried, rest = refs[: 3 if begin else 0], refs[3 if begin else 0 :]
    outs, (key_t, key_sum, value_sum) = rest[:-3], rest[-3:]
    query_g = outs[0]

    @pl.loop(0, blocks)
    def _(index):
        key_t[index] = key[block_rows(index), :].T
        if begin:
            key_sum[block_rows(index), :] = carried[1][block_rows(index), :]
            value_sum[block_rows(index), :] = carried[2][block_rows(index), :]
        else:
            key_sum[block_rows(index), :] = jnp.zeros((BLK, PAIR), jnp.float32)
            value_sum[block_rows(index), :] = jnp.zeros((BLK, PAIR), jnp.float32)

    def query_block(index, slots):
        picked = [adjacency[index, slot] for slot in range(slots)]
        query_rows = query[block_rows(index), :]
        grad_rows = grad[block_rows(index), :]
        queries, queries_t = by_head(query_rows), by_head_t(query_rows)
        grads, grads_t = by_head(grad_rows), by_head_t(grad_rows)
        stat = stats[0, pl.ds(pl.multiple_of(index * 8, 8), 1), :]
        products = (
            grad_rows.astype(jnp.float32) * attn_out[block_rows(index), :].astype(jnp.float32)
        ).T
        row_dot = jnp.concatenate(
            [
                jnp.sum(products[:HD], axis=0, keepdims=True),
                jnp.sum(products[HD:], axis=0, keepdims=True),
            ],
            axis=1,
        )
        places = [block_rows(block) for block in picked]
        prob = jnp.exp2(stack(key, places, queries_t) * BASE2 - stat)
        term = (prob * (stack(value, places, grads_t) - row_dot)).astype(jnp.bfloat16)
        key_terms = dot(term, queries)
        value_terms = dot(prob.astype(jnp.bfloat16), grads)
        for number, at in enumerate(places):
            key_sum[at, :] += key_terms[BLK * number : BLK * (number + 1)]
            value_sum[at, :] += value_terms[BLK * number : BLK * (number + 1)]
        query_t = dot(jnp.concatenate([key_t[block] for block in picked], axis=1), term)
        query_g[block_rows(index), :PAIR] = (own_parts(query_t).T * SCALE).astype(jnp.bfloat16)

    each_block(counts, begin, end, 1, query_block)
    if end < blocks:
        outs[1][...], outs[2][...] = key_sum[...], value_sum[...]
    else:
        if begin:
            query_g[: BLK * begin, :PAIR] = carried[0][: BLK * begin, :]
        query_g[:, PAIR : 2 * PAIR] = (key_sum[...] * SCALE).astype(jnp.bfloat16)
        query_g[:, 2 * PAIR :] = value_sum[...].astype(jnp.bfloat16)


VMEM = pl.BlockSpec(memory_space=pltpu.VMEM)
SMEM = pl.BlockSpec(memory_space=pltpu.SMEM)
SMALL = pltpu.CompilerParams(vmem_limit_bytes=16 * 2**20)
PARAMS = pltpu.CompilerParams(vmem_limit_bytes=32 * 2**20)
WIDE = pltpu.CompilerParams(vmem_limit_bytes=60 * 2**20)


def cost(tokens, products):
    tiles = tokens // BLK * MAXK * 2
    return pl.CostEstimate(
        flops=tiles * products * 2 * BLK * BLK * HD * 4,
        bytes_accessed=12 * tokens * PAIR,
        transcendentals=tiles * BLK * BLK,
    )


def forward(packed, adjacency, counts, begin, end, carried=()):
    tokens = packed.shape[0]
    blocks = tokens // BLK
    return pl.pallas_call(
        functools.partial(forward_kernel, begin=begin, end=end),
        in_specs=[SMEM, SMEM, VMEM] + [VMEM] * len(carried),
        out_specs=[VMEM] * 3,
        out_shape=[
            jax.ShapeDtypeStruct((tokens, PAIR), jnp.bfloat16),
            jax.ShapeDtypeStruct((tokens, PAIR), jnp.bfloat16),
            jax.ShapeDtypeStruct((2, blocks * 8, 2 * BLK), jnp.float32),
        ],
        scratch_shapes=[pltpu.VMEM((2, blocks, PAIR, BLK), jnp.bfloat16)],
        compiler_params=PARAMS,
        cost_estimate=cost(tokens * (end - begin) // blocks, 4),
        name="attend_forward",
    )(adjacency, counts, packed, *carried)


def backward(packed, grad, pair, attn_out, stats, adjacency, counts, begin=0, end=None, carried=()):
    tokens = packed.shape[0]
    blocks = tokens // BLK
    end = end or blocks
    one = pl.BlockSpec((tokens, PAIR), lambda step: (0, 0))
    three = pl.BlockSpec((tokens, 3 * PAIR), lambda step: (0, pair))
    whole = pl.BlockSpec((tokens, 3 * PAIR), lambda step: (0, 0))
    if end < blocks:
        out_specs = [one] * 3
        out_shape = [jax.ShapeDtypeStruct((tokens, PAIR), jnp.bfloat16)]
        out_shape += [jax.ShapeDtypeStruct((tokens, PAIR), jnp.float32)] * 2
    else:
        out_specs = whole
        out_shape = jax.ShapeDtypeStruct((tokens, 3 * PAIR), jnp.bfloat16)
    return pl.pallas_call(
        functools.partial(backward_kernel, blocks=blocks, begin=begin, end=end),
        grid=(1,),
        in_specs=[
            SMEM, SMEM, three, pl.BlockSpec((tokens, PAIR), lambda step: (0, pair)), one,
            pl.BlockSpec((1, blocks * 8, 2 * BLK), lambda step: (pair, 0, 0)),
        ] + [one] * len(carried),
        out_specs=out_specs,
        out_shape=out_shape,
        scratch_shapes=[
            pltpu.VMEM((blocks, PAIR, BLK), jnp.bfloat16),
            pltpu.VMEM((tokens, PAIR), jnp.float32),
            pltpu.VMEM((tokens, PAIR), jnp.float32),
        ],
        compiler_params=WIDE,
        cost_estimate=cost(tokens * (end - begin) // blocks, 5),
        name="attend_backward",
    )(adjacency, counts, packed, grad, attn_out, stats, *carried)


STEPS = 4


def pack_kernel(queries, keys, values, out_grad, weight, packed, top, bottom, own):
    step = pl.program_id(0)
    for group in range(packed.shape[0]):
        for pair in range(2):
            start = PAIR * (2 * group + pair)
            for part, source in enumerate((queries, keys, values)):
                packed[group, :, columns(pair, part)] = source[:, start : start + PAIR]
    own[...] = weight[...]

    @pl.when(step < STEPS // 2)
    def _():
        top[...] = out_grad[...]

    @pl.when(step >= STEPS // 2)
    def _():
        bottom[...] = out_grad[...]


def pack(queries, keys, values, out_grad, out_weight, groups):
    tokens, width = queries.shape
    height, middle = tokens // STEPS, STEPS // 2
    share = width // groups // STEPS

    def weight_place(step):
        skipped = lax.axis_index("seq") * (width // groups) % out_weight.shape[0]
        return (skipped // share + step, 0)

    taken = pl.BlockSpec((height, width), lambda step: (step, 0))
    return pl.pallas_call(
        pack_kernel,
        grid=(STEPS,),
        in_specs=[taken] * 4 + [pl.BlockSpec((share, width), weight_place)],
        out_specs=[
            pl.BlockSpec((groups, height, 6 * PAIR), lambda step: (0, step, 0)),
            pl.BlockSpec((height, width), lambda step: (jnp.minimum(step, middle - 1), 0)),
            pl.BlockSpec((height, width), lambda step: (jnp.maximum(step - middle, 0), 0)),
            pl.BlockSpec((share, width), lambda step: (step, 0)),
        ],
        out_shape=[
            jax.ShapeDtypeStruct((groups, tokens, 6 * PAIR), queries.dtype),
            jax.ShapeDtypeStruct((tokens // 2, width), queries.dtype),
            jax.ShapeDtypeStruct((tokens // 2, width), queries.dtype),
            jax.ShapeDtypeStruct((width // groups, width), queries.dtype),
        ],
        compiler_params=WIDE,
        name="pack",
    )(queries, keys, values, out_grad, out_weight)


def unpack_kernel(first, second, query_g, key_g, value_g):
    for group in range(first.shape[0]):
        for pair, source in enumerate((first, second)):
            start = PAIR * (2 * group + pair)
            for part, out in enumerate((query_g, key_g, value_g)):
                out[:, start : start + PAIR] = source[group, :, PAIR * part : PAIR * (part + 1)]


def unpack(first, second):
    groups, tokens, _ = first.shape
    height = tokens // 4
    taken = pl.BlockSpec((groups, height, 3 * PAIR), lambda step: (0, step, 0))
    given = pl.BlockSpec((height, groups * 2 * PAIR), lambda step: (step, 0))
    return pl.pallas_call(
        unpack_kernel,
        grid=(4,),
        in_specs=[taken] * 2,
        out_specs=[given] * 3,
        out_shape=[jax.ShapeDtypeStruct((tokens, groups * 2 * PAIR), first.dtype)] * 3,
        compiler_params=SMALL,
        name="unpack",
    )(first, second)


def spread_kernel(*refs):
    pieces, out = refs[:-1], refs[-1]
    member = lax.axis_index("seq")
    for mask, piece in enumerate(pieces):
        width = piece.shape[1]
        start = pl.multiple_of((member ^ mask) * width, width)
        out[:, pl.ds(start, width)] = piece[...].astype(out.dtype)


def spread(pieces):
    rows, width = pieces[0].shape
    height = rows // STEPS
    return pl.pallas_call(
        spread_kernel,
        grid=(STEPS,),
        in_specs=[pl.BlockSpec((height, width), lambda step: (step, 0))] * len(pieces),
        out_specs=pl.BlockSpec((height, len(pieces) * width), lambda step: (step, 0)),
        out_shape=jax.ShapeDtypeStruct((rows, len(pieces) * width), jnp.float32),
        compiler_params=WIDE,
        name="spread",
    )(*pieces)


def exchange(chunks):
    return lax.all_to_all(chunks, "seq", split_axis=0, concat_axis=0, tiled=True)


WEIGHT_ROUTES = (
    ((0, 1), (1, 2), (2, 1), (3, 2)),
    ((0, 2), (1, 3), (2, 0), (3, 1)),
    ((2, 3), (1, 0), (2, 3), (1, 0)),
)


def send_weight(rows, step):
    planes, members = lax.axis_size("fsdp"), lax.axis_size("seq")
    routes = []
    for member in range(members):
        source, target = WEIGHT_ROUTES[step][member * planes // members]
        routes.append((source * members + member, target * members + member))
    return lax.ppermute(rows, ("fsdp", "seq"), routes)


def swap(array, mask):
    routes = [(s, s ^ mask) for s in range(lax.axis_size("seq"))]
    return lax.ppermute(array, "seq", routes)


def project_kernel(places, *refs):
    pieces, rest = refs[: len(places)], refs[len(places) :]
    weights, (first, second, attn_grad, terms) = rest[:4], rest[4:8]
    whole, weight, weight_t, landed, fetched = rest[8:]
    plane, member = lax.axis_index("fsdp"), lax.axis_index("seq")
    local = whole.shape[0] // terms.shape[0]
    copies = []
    for number, (mask, row) in enumerate(places):
        start = pl.multiple_of((member ^ mask) * local + row, BLK)
        target = whole.at[pl.ds(start, pieces[number].shape[0]), :]
        copies.append(pltpu.make_async_copy(pieces[number], target, landed.at[number]))
    for source, rows in enumerate(weights):
        held = (plane == member // 2) if source == 0 else False
        for home, (_, target) in enumerate(WEIGHT_ROUTES[source - 1] if source else ()):
            held = held | ((member // 2 == home) & (plane == target))

        @pl.when(held)
        def _():
            pltpu.make_async_copy(rows, weight, fetched).start()
    for copy in copies:
        copy.start()
    pltpu.make_async_copy(weights[0], weight, fetched).wait()
    weight_t[...] = weight[...].T
    attn_t = jnp.concatenate([first[...].T, second[...].T], axis=0)
    for copy in copies:
        copy.wait()
    groups, _, width = terms.shape
    for group in range(0, groups, 2):
        wide = dot(attn_t, whole[:, width * group : width * (group + 2)]).astype(terms.dtype)
        terms[group], terms[group + 1] = wide[:, :width], wide[:, width:]

    @pl.loop(0, 4)
    def _(part):
        rows = block_rows(part, whole.shape[0] // 4)
        attn_grad[rows, :] = dot(whole[rows, :], weight_t[...]).astype(attn_grad.dtype)


def project(pieces, weights, first, second, groups):
    places = [(mask, row) for mask, row, _ in pieces]
    arrays = [piece for _, _, piece in pieces]
    height, width = weights[0].shape
    tokens = first.shape[0]
    far = pl.BlockSpec(memory_space=pl.ANY)
    return pl.pallas_call(
        functools.partial(project_kernel, places),
        in_specs=[far] * (len(arrays) + len(weights)) + [VMEM] * 2,
        out_specs=[VMEM] * 2,
        out_shape=[
            jax.ShapeDtypeStruct((tokens, height), jnp.bfloat16),
            jax.ShapeDtypeStruct((groups, height, width // groups), jnp.bfloat16),
        ],
        scratch_shapes=[
            pltpu.VMEM((tokens, width), jnp.bfloat16),
            pltpu.VMEM((height, width), jnp.bfloat16),
            pltpu.VMEM((width, height), jnp.bfloat16),
            pltpu.SemaphoreType.DMA((len(arrays),)),
            pltpu.SemaphoreType.DMA,
        ],
        compiler_params=PARAMS,
        cost_estimate=pl.CostEstimate(
            flops=4 * tokens * width * height,
            bytes_accessed=2 * tokens * width + 8 * height * width,
            transcendentals=0,
        ),
        name="project",
    )(*arrays, *weights, first, second)


def split_kernel(whole, *parts):
    height = parts[0].shape[0]
    for offset, part in enumerate(parts):
        start = pl.multiple_of((lax.axis_index("fsdp") ^ offset) * height, height)
        part[...] = whole[pl.ds(start, height), :]


def split(whole, planes):
    rows, width = whole.shape
    return pl.pallas_call(
        split_kernel,
        in_specs=[VMEM],
        out_specs=[VMEM] * planes,
        out_shape=[jax.ShapeDtypeStruct((rows // planes, width), whole.dtype)] * planes,
        compiler_params=PARAMS,
        name="split",
    )(whole)


def fits_pairs(sizes):
    planes, members = sizes["fsdp"], sizes["seq"]
    return members == 8 and planes == 4 and members * 2 * PAIR == HEADS * HD


def pair_device(queries, keys, values, out_grad, out_weight, key_blocks, block_counts):
    planes, members = lax.axis_size("fsdp"), lax.axis_size("seq")
    home = lax.axis_index("seq") // 2
    local_tokens, model_width = queries.shape[1:]
    tokens = local_tokens * members
    adjacency, counts = key_blocks[0], block_counts[0]
    shard = out_grad[0]

    chunks, top, bottom, own = pack(queries[0], keys[0], values[0], shard, out_weight, members)
    packed = exchange(chunks).reshape(tokens, 6 * PAIR)
    near, far = send_weight(own, 0), send_weight(own, 1)
    beside = swap(shard, 1)
    packed, shard, top, bottom, near, beside = lax.optimization_barrier(
        (packed, shard, top, bottom, near, beside)
    )

    along = swap(top, 2), swap(bottom, 2)
    across = swap(top, 4), swap(bottom, 4)
    blocks = tokens // BLK
    done = forward(packed, adjacency, counts, 0, blocks // 2)
    done, far = lax.optimization_barrier((done, far))
    last = send_weight(jnp.where((home == 1) | (home == 2), own, far), 2)
    done = forward(packed, adjacency, counts, blocks // 2, blocks, done)
    (first, second, stats), along, across = lax.optimization_barrier((done, along, across))

    halves = list(zip((2, 2, 4, 4, 6, 6), (0, 1) * 3, (*along, *across, swap(along[0], 4), swap(across[1], 2))))
    pieces = [(0, 0, shard), (1, 0, beside)]
    for mask, half, piece in halves:
        row = half * local_tokens // 2
        pieces += [(mask, row, piece), (mask ^ 1, row, swap(piece, 1))]
    attn_grad, by_columns = project(pieces, (own, near, far, last), first, second, members)

    terms = exchange(by_columns).reshape(model_width, -1)
    first_g = backward(packed, attn_grad, 0, first, stats, adjacency, counts)
    first_g, terms = lax.optimization_barrier((first_g, terms))
    parts = split(terms, planes)
    received = [
        lax.ppermute(parts[offset], "fsdp", [(z, z ^ offset) for z in range(planes)])
        for offset in range(1, planes)
    ]
    first_r = exchange(first_g.reshape(members, local_tokens, 3 * PAIR))
    split_at = tokens // BLK * 11 // 16
    started = backward(
        packed, attn_grad, 1, second, stats, adjacency, counts, end=split_at
    )
    *started, received = lax.optimization_barrier((*started, received))
    summed = sum(part.astype(jnp.float32) for part in [parts[0], *received]).astype(terms.dtype)
    sides = [summed, swap(summed, 2), swap(summed, 4), swap(summed, 6)]
    second_g = backward(
        packed, attn_grad, 1, second, stats, adjacency, counts, begin=split_at, carried=started
    )
    second_g, *sides = lax.optimization_barrier((second_g, *sides))
    wo_grad = spread([part for one in sides for part in (one, swap(one, 1))])
    second_r = exchange(second_g.reshape(members, local_tokens, 3 * PAIR))
    query_g, key_g, value_g = unpack(first_r, second_r)
    return (query_g[None], key_g[None], value_g[None], wo_grad)


def general_device(queries, keys, values, out_grad, out_weight, key_blocks, block_counts):
    local_tokens = queries.shape[1]
    model_width = queries.shape[2]
    seq_devices = lax.axis_size("seq")
    loss_grad = out_grad[0]
    adjacency = key_blocks[0]
    slot_live = jnp.arange(MAXK)[None, :] < block_counts[0][:, None]

    def head_groups(array):
        return array[0].reshape(local_tokens, seq_devices, HEADS // seq_devices, HD)

    attn_grad = lax.dot_general(
        loss_grad,
        lax.all_gather(out_weight, "fsdp", axis=0, tiled=True),
        (((1,), (1,)), ((), ())),
        preferred_element_type=jnp.float32,
    ).astype(jnp.bfloat16)

    def attend(heads_in):
        query_h, key_h, value_h, grad_h = (member[:, 0] for member in heads_in)
        row_max, row_sum, attn_blocks = head_forward(query_h, key_h, value_h, adjacency, slot_live)
        query_g, key_g, value_g = head_backward(
            query_h, key_h, value_h, grad_h, row_max, row_sum, attn_blocks, adjacency, slot_live
        )
        return (query_g, key_g, value_g, attn_blocks.reshape(-1, query_h.shape[1], HD))

    query_g, key_g, value_g, attn_heads = attend(
        (
            lax.all_to_all(head_groups(queries), "seq", split_axis=1, concat_axis=0, tiled=True),
            lax.all_to_all(head_groups(keys), "seq", split_axis=1, concat_axis=0, tiled=True),
            lax.all_to_all(head_groups(values), "seq", split_axis=1, concat_axis=0, tiled=True),
            lax.all_to_all(
                head_groups(attn_grad[None]), "seq", split_axis=1, concat_axis=0, tiled=True
            ),
        )
    )
    query_t, key_t, value_t, attn_t = (
        lax.all_to_all(query_g, "seq", split_axis=0, concat_axis=1, tiled=True),
        lax.all_to_all(key_g, "seq", split_axis=0, concat_axis=1, tiled=True),
        lax.all_to_all(value_g, "seq", split_axis=0, concat_axis=1, tiled=True),
        lax.all_to_all(attn_heads, "seq", split_axis=0, concat_axis=1, tiled=True),
    )
    attn_out = attn_t.reshape(local_tokens, model_width)
    share = lax.psum_scatter(
        lax.dot_general(
            attn_out, loss_grad, (((0,), (0,)), ((), ())), preferred_element_type=jnp.float32
        ),
        ("fsdp", "seq"),
        scatter_dimension=0,
        tiled=True,
    )
    wo_grad = lax.all_gather(share.astype(jnp.bfloat16), "seq", axis=0, tiled=True).astype(
        share.dtype
    )

    def to_tokens(array):
        return array.reshape(1, local_tokens, model_width)

    return (to_tokens(query_t), to_tokens(key_t), to_tokens(value_t), wo_grad)


def on_device(mesh):
    return pair_device if fits_pairs(mesh.shape) else general_device


def solution(mesh):
    return jax.shard_map(
        on_device(mesh),
        mesh=mesh,
        in_specs=(
            P("fsdp", "seq", None),
            P("fsdp", "seq", None),
            P("fsdp", "seq", None),
            P("fsdp", "seq", None),
            P("fsdp", None),
            P("fsdp", None, None),
            P("fsdp", None),
        ),
        out_specs=(
            P("fsdp", "seq", None),
            P("fsdp", "seq", None),
            P("fsdp", "seq", None),
            P("fsdp", None),
        ),
        check_vma=False,
    )
```

profile of v0, /device:TPU:16, one launch (start us, length us, event | category | flops | bytes accessed | tf_op | source)
XLA Modules:
  0.0 201.1 jit_solution(1138417674625752774)
XLA Ops:
  0.6 5.4 %pack.1 = (bf16[8,256,768]{2,1,0:T(8,128)(2,1)}, bf16[128,2048]{1,0:T(8,128)(2,1)}, bf16[128,2048]{1,0:T(8,128)(2,1)}, bf16[256,2048]{1,0:T(8,128)(2,1)}) custom-call(bf16[256,2048]{1,0:T(8,128)(2,1)} %bitcast.34, bf16[256,2048]{1,0:T(8,128)(2,1)} %bitcast.35, bf16[256,2048]{1,0:T(8,128)(2,1)} %bitcast.36, bf16[256,2048]{1,0:T(8,128)(2,1)} %bitcast.19, ...), custom_call_target="tpu_custom_call" | custom-call | tf_op jit(solution)/shard_map/pack/pallas_call | solution.py:372
  6.0 3.9 %all-to-all-start = ((bf16[8,256,768]{2,1,0:T(8,128)(2,1)}), bf16[8,256,768]{2,1,0:T(8,128)(2,1)S(1)}, u32[]{:S(2)}, u32[]{:S(2)}) async-start(bf16[8,256,768]{2,1,0:T(8,128)(2,1)} %get-tuple-element.56), calls=%async_computation | async-start | bytes 6291456 | tf_op jit(solution)/shard_map/all_to_all | solution.py:441
  10.4 1.6 collective-permute-start
  13.5 34.3 %all-to-all-done = bf16[8,256,768]{2,1,0:T(8,128)(2,1)S(1)} async-done(((bf16[8,256,768]{2,1,0:T(8,128)(2,1)}), bf16[8,256,768]{2,1,0:T(8,128)(2,1)S(1)}, u32[]{:S(2)}, u32[]{:S(2)}) %all-to-all-start) | async-done | bytes 3145760 | tf_op jit(solution)/shard_map/all_to_all | solution.py:441
  50.3 1.5 collective-permute-start.4
  51.9 10.3 %attend_forward.2 = (bf16[2048,128]{1,0:T(8,128)(2,1)S(1)}, bf16[2048,128]{1,0:T(8,128)(2,1)S(1)}, f32[2,128,256]{2,1,0:T(8,128)S(1)}) custom-call(s32[16,10]{1,0:T(8,128)S(1)} %bitcast.22, s32[16]{0:T(128)S(1)} %bitcast.30, bf16[2048,768]{1,0:T(8,128)(2,1)S(1)} %bitcast.14), custom_call_target="tpu_custom_call" | custom-call | flops 5368709120 | bytes 1572864 | tf_op jit(solution)/shard_map/attend_forward/pallas_call | solution.py:291
  63.5 4.8 %collective-permute-start.15 = (bf16[256,2048]{1,0:T(8,128)(2,1)S(1)}, bf16[256,2048]{1,0:T(8,128)(2,1)S(1)}, u32[]{:S(2)}, u32[]{:S(2)}) collective-permute-start(bf16[256,2048]{1,0:T(8,128)(2,1)S(1)} %broadcast_select_fusion), channel_id=1, source_target_pairs={{16,24},{17,25},{10,2},{11,3},{20,28},{21,29},{14,6},{15,7}} | collective-permute-start | bytes 3145736 | tf_op jit(solution)/shard_map/ppermute | solution.py:457
  68.4 10.8 %attend_forward.3 = (bf16[2048,128]{1,0:T(8,128)(2,1)S(1)}, bf16[2048,128]{1,0:T(8,128)(2,1)S(1)}, f32[2,128,256]{2,1,0:T(8,128)S(1)}) custom-call(s32[16,10]{1,0:T(8,128)S(1)} %bitcast.23, s32[16]{0:T(128)S(1)} %bitcast.31, bf16[2048,768]{1,0:T(8,128)(2,1)S(1)} %bitcast.15, bf16[2048,128]{1,0:T(8,128)(2,1)S(1)} %get-tuple-element.66.refs_0_, ...), custom_call_target="tpu_custom_call" | custom-call | flops 5368709120 | bytes 1572864 | tf_op jit(solution)/shard_map/attend_forward/pallas_call | solution.py:291
  80.5 1.4 collective-permute-done.8.refs_5_
  82.7 11.6 %collective-permute-done.11.refs_10_ = bf16[128,2048]{1,0:T(8,128)(2,1)S(1)} collective-permute-done((bf16[128,2048]{1,0:T(8,128)(2,1)S(1)}, bf16[128,2048]{1,0:T(8,128)(2,1)S(1)}, u32[]{:S(2)}, u32[]{:S(2)}) %collective-permute-start.11) | collective-permute-done | bytes 524320 | tf_op jit(solution)/shard_map/ppermute | solution.py:462
  97.0 7.4 %project.1 = (bf16[2048,256]{1,0:T(8,128)(2,1)S(1)}, bf16[8,256,256]{2,1,0:T(8,128)(2,1)}) custom-call(bf16[256,2048]{1,0:T(8,128)(2,1)S(1)} %bitcast.21, bf16[256,2048]{1,0:T(8,128)(2,1)} %collective-permute-done.1.refs_1_, bf16[128,2048]{1,0:T(8,128)(2,1)S(1)} %collective-permute-done.3.refs_2_, bf16[128,2048]{1,0:T(8,128)(2,1)S(1)} %collective-permute-done.7.refs_3_, ...), custom_call_target="tpu_custom_call" | custom-call | flops 4294967296 | bytes 12582912 | tf_op jit(solution)/shard_map/project/pallas_call | solution.py:508
  105.5 3.7 %all-to-all-start.1 = ((bf16[8,256,256]{2,1,0:T(8,128)(2,1)}), bf16[8,256,256]{2,1,0:T(8,128)(2,1)S(1)}, u32[]{:S(2)}, u32[]{:S(2)}) async-start(bf16[8,256,256]{2,1,0:T(8,128)(2,1)} %get-tuple-element.84), calls=%async_computation.1 | async-start | bytes 2097152 | tf_op jit(solution)/shard_map/all_to_all | solution.py:441
  109.2 17.5 %attend_backward.3 = bf16[2048,384]{1,0:T(8,128)(2,1)} custom-call(s32[16,10]{1,0:T(8,128)} %bitcast.24, s32[16]{0:T(128)} %bitcast.27, bf16[2048,768]{1,0:T(8,128)(2,1)} %bitcast.16, bf16[2048,256]{1,0:T(8,128)(2,1)} %copy-done.5, bf16[2048,128]{1,0:T(8,128)(2,1)} %copy-done.7, f32[2,128,256]{2,1,0:T(8,128)} %copy-done.8), custom_call_target="tpu_custom_call" | custom-call | flops 13421772800 | bytes 3145728 | tf_op jit(solution)/shard_map/attend_backward/pallas_call | solution.py:321
  126.7 4.1 %all-to-all-start.2 = ((bf16[8,256,384]{2,1,0:T(8,128)(2,1)}), bf16[8,256,384]{2,1,0:T(8,128)(2,1)S(1)}, u32[]{:S(2)}, u32[]{:S(2)}) async-start(bf16[8,256,384]{2,1,0:T(8,128)(2,1)} %bitcast.32), calls=%async_computation.2 | async-start | bytes 3145728 | tf_op jit(solution)/shard_map/all_to_all | solution.py:441
  131.0 3.4 %collective-permute-start.18 = (bf16[512,256]{1,0:T(8,128)(2,1)S(1)}, bf16[512,256]{1,0:T(8,128)(2,1)S(1)}, u32[]{:S(2)}, u32[]{:S(2)}) collective-permute-start(bf16[512,256]{1,0:T(8,128)(2,1)S(1)} %get-tuple-element.92), channel_id=1, source_target_pairs={{0,24},{8,16},{16,8},{24,0},{1,25},{9,17},{17,9},{25,1},{2,26},{10... | collective-permute-start | bytes 786440 | tf_op jit(solution)/shard_map/ppermute | solution.py:594
  134.4 13.6 %attend_backward.4 = (bf16[2048,128]{1,0:T(8,128)(2,1)}, f32[2048,128]{1,0:T(8,128)}, f32[2048,128]{1,0:T(8,128)}) custom-call(s32[16,10]{1,0:T(8,128)} %bitcast.25, s32[16]{0:T(128)} %bitcast.28, bf16[2048,768]{1,0:T(8,128)(2,1)} %bitcast.17, bf16[2048,256]{1,0:T(8,128)(2,1)} %copy-done.5, bf16[2048,128]{1,0:T(8,128)(2,1)} %copy-done.6, ...), custom_call_target="tpu_custom_call" | custom-call | flops 9227468800 | bytes 2162688 | tf_op jit(solution)/shard_map/attend_backward/pallas_call | solution.py:321
  148.0 9.5 %collective-permute-done.18 = bf16[512,256]{1,0:T(8,128)(2,1)S(1)} collective-permute-done((bf16[512,256]{1,0:T(8,128)(2,1)S(1)}, bf16[512,256]{1,0:T(8,128)(2,1)S(1)}, u32[]{:S(2)}, u32[]{:S(2)}) %collective-permute-start.18) | collective-permute-done | bytes 262176 | tf_op jit(solution)/shard_map/ppermute | solution.py:594
  157.6 2.6 %collective-permute-start.21 = (bf16[512,256]{1,0:T(8,128)(2,1)S(1)}, bf16[512,256]{1,0:T(8,128)(2,1)S(1)}, u32[]{:S(2)}, u32[]{:S(2)}) collective-permute-start(bf16[512,256]{1,0:T(8,128)(2,1)S(1)} %add_convert_fusion.refs_0_), channel_id=1, source_target_pairs={{0,6},{1,7},{2,4},{3,5},{4,2},{5,3},{6,0},{7,1},{8,14},{9,15},{10,... | collective-permute-start | bytes 786440 | tf_op jit(solution)/shard_map/ppermute | solution.py:462
  161.2 9.3 %attend_backward.5 = bf16[2048,384]{1,0:T(8,128)(2,1)} custom-call(s32[16,10]{1,0:T(8,128)} %bitcast.26, s32[16]{0:T(128)} %bitcast.29, bf16[2048,768]{1,0:T(8,128)(2,1)} %bitcast.18, bf16[2048,256]{1,0:T(8,128)(2,1)} %copy-done.5, bf16[2048,128]{1,0:T(8,128)(2,1)} %copy-done.6, f32[2,128,256]{2,1,0:T(8,128)} %copy-done.8, ...), custom_call_target="tpu_custom_call" | custom-call | flops 4194304000 | bytes 983040 | tf_op jit(solution)/shard_map/attend_backward/pallas_call | solution.py:321
  170.5 2.0 %collective-permute-done.20.refs_4_ = bf16[512,256]{1,0:T(8,128)(2,1)S(1)} collective-permute-done((bf16[512,256]{1,0:T(8,128)(2,1)S(1)}, bf16[512,256]{1,0:T(8,128)(2,1)S(1)}, u32[]{:S(2)}, u32[]{:S(2)}) %collective-permute-start.20) | collective-permute-done | bytes 262176 | tf_op jit(solution)/shard_map/ppermute | solution.py:462
  173.9 3.6 %all-to-all-start.3 = ((bf16[8,256,384]{2,1,0:T(8,128)(2,1)}), bf16[8,256,384]{2,1,0:T(8,128)(2,1)S(1)}, u32[]{:S(2)}, u32[]{:S(2)}) async-start(bf16[8,256,384]{2,1,0:T(8,128)(2,1)} %bitcast.33), calls=%async_computation.3 | async-start | bytes 3145728 | tf_op jit(solution)/shard_map/all_to_all | solution.py:441
  180.6 4.2 %spread.1 = f32[512,2048]{1,0:T(8,128)} custom-call(bf16[512,256]{1,0:T(8,128)(2,1)} %copy-done.9, bf16[512,256]{1,0:T(8,128)(2,1)} %copy-done.13, bf16[512,256]{1,0:T(8,128)(2,1)} %copy-done.12, bf16[512,256]{1,0:T(8,128)(2,1)} %copy-done.14, bf16[512,256]{1,0:T(8,128)(2,1)} %copy-done.11, bf16[512,256]{1,0:T(8,128)(2,1)} %collective-permute-done.24.refs_5_, ...), custom_call_target="tpu_custom_call" | custom-call | tf_op jit(solution)/shard_map/spread/pallas_call | solution.py:429
  184.8 13.6 %all-to-all-done.3.second = bf16[8,256,384]{2,1,0:T(8,128)(2,1)S(1)} async-done(((bf16[8,256,384]{2,1,0:T(8,128)(2,1)}), bf16[8,256,384]{2,1,0:T(8,128)(2,1)S(1)}, u32[]{:S(2)}, u32[]{:S(2)}) %all-to-all-start.3) | async-done | bytes 1572896 | tf_op jit(solution)/shard_map/all_to_all | solution.py:441
  198.4 2.7 %unpack.1 = (bf16[256,2048]{1,0:T(8,128)(2,1)}, bf16[256,2048]{1,0:T(8,128)(2,1)}, bf16[256,2048]{1,0:T(8,128)(2,1)}) custom-call(bf16[8,256,384]{2,1,0:T(8,128)(2,1)S(1)} %all-to-all-done.2.first, bf16[8,256,384]{2,1,0:T(8,128)(2,1)S(1)} %all-to-all-done.3.second), custom_call_target="tpu_custom_call" | custom-call | tf_op jit(solution)/shard_map/unpack/pallas_call | solution.py:406
  (81 shorter events, 17.4 us)
Async XLA Ops:
  6.0 41.8 %all-to-all-start = ((bf16[8,256,768]{2,1,0:T(8,128)(2,1)}), bf16[8,256,768]{2,1,0:T(8,128)(2,1)S(1)}, u32[]{:S(2)}, u32[]{:S(2)}) async-start(bf16[8,256,768]{2,1,0:T(8,128)(2,1)} %get-tuple-element.56), calls=%async_computation | async-start | bytes 6291456 | tf_op jit(solution)/shard_map/all_to_all | solution.py:441
  9.9 3.6 %collective-permute-start.1 = (bf16[256,2048]{1,0:T(8,128)(2,1)}, bf16[256,2048]{1,0:T(8,128)(2,1)}, u32[]{:S(2)}, u32[]{:S(2)}) collective-permute-start(bf16[256,2048]{1,0:T(8,128)(2,1)} %bitcast.20), channel_id=1, source_target_pairs={{0,1},{1,0},{2,3},{3,2},{4,5},{5,4},{6,7},{7,6},{8,9},{9,8},{10,11... | collective-permute-start | bytes 3145736 | tf_op jit(solution)/shard_map/ppermute | solution.py:462
  10.4 3.1 %collective-permute-start = (bf16[256,2048]{1,0:T(8,128)(2,1)}, bf16[256,2048]{1,0:T(8,128)(2,1)}, u32[]{:S(2)}, u32[]{:S(2)}) collective-permute-start(bf16[256,2048]{1,0:T(8,128)(2,1)} %get-tuple-element.59.refs_14_), channel_id=1, source_target_pairs={{0,8},{1,9},{10,18},{11,19},{20,12},{21,13},{30,22},{31,23}} | collective-permute-start | bytes 3145736 | tf_op jit(solution)/shard_map/ppermute | solution.py:457
  12.0 50.1 %collective-permute-start.2 = (bf16[256,2048]{1,0:T(8,128)(2,1)}, bf16[256,2048]{1,0:T(8,128)(2,1)}, u32[]{:S(2)}, u32[]{:S(2)}) collective-permute-start(bf16[256,2048]{1,0:T(8,128)(2,1)} %get-tuple-element.59.refs_14_), channel_id=1, source_target_pairs={{0,16},{1,17},{10,26},{11,27},{20,4},{21,5},{30,14},{31,15}} | collective-permute-start | bytes 3145736 | tf_op jit(solution)/shard_map/ppermute | solution.py:457
  47.8 32.1 %collective-permute-start.5 = (bf16[128,2048]{1,0:T(8,128)(2,1)}, bf16[128,2048]{1,0:T(8,128)(2,1)S(1)}, u32[]{:S(2)}, u32[]{:S(2)}) collective-permute-start(bf16[128,2048]{1,0:T(8,128)(2,1)} %get-tuple-element.72), channel_id=1, source_target_pairs={{0,4},{1,5},{2,6},{3,7},{4,0},{5,1},{6,2},{7,3},{8,12},{9,13},{10,... | collective-permute-start | bytes 1572872 | tf_op jit(solution)/shard_map/ppermute | solution.py:462
  48.3 31.5 %collective-permute-start.3 = (bf16[128,2048]{1,0:T(8,128)(2,1)}, bf16[128,2048]{1,0:T(8,128)(2,1)S(1)}, u32[]{:S(2)}, u32[]{:S(2)}) collective-permute-start(bf16[128,2048]{1,0:T(8,128)(2,1)} %get-tuple-element.72), channel_id=1, source_target_pairs={{0,2},{1,3},{2,0},{3,1},{4,6},{5,7},{6,4},{7,5},{8,10},{9,11},{10,... | collective-permute-start | bytes 1572872 | tf_op jit(solution)/shard_map/ppermute | solution.py:462
  48.9 30.9 %collective-permute-start.6 = (bf16[128,2048]{1,0:T(8,128)(2,1)}, bf16[128,2048]{1,0:T(8,128)(2,1)S(1)}, u32[]{:S(2)}, u32[]{:S(2)}) collective-permute-start(bf16[128,2048]{1,0:T(8,128)(2,1)} %get-tuple-element.73), channel_id=1, source_target_pairs={{0,4},{1,5},{2,6},{3,7},{4,0},{5,1},{6,2},{7,3},{8,12},{9,13},{10,... | collective-permute-start | bytes 1572872 | tf_op jit(solution)/shard_map/ppermute | solution.py:462
  50.3 29.6 %collective-permute-start.4 = (bf16[128,2048]{1,0:T(8,128)(2,1)}, bf16[128,2048]{1,0:T(8,128)(2,1)S(1)}, u32[]{:S(2)}, u32[]{:S(2)}) collective-permute-start(bf16[128,2048]{1,0:T(8,128)(2,1)} %get-tuple-element.73), channel_id=1, source_target_pairs={{0,2},{1,3},{2,0},{3,1},{4,6},{5,7},{6,4},{7,5},{8,10},{9,11},{10,... | collective-permute-start | bytes 1572872 | tf_op jit(solution)/shard_map/ppermute | solution.py:462
  63.5 31.3 %collective-permute-start.15 = (bf16[256,2048]{1,0:T(8,128)(2,1)S(1)}, bf16[256,2048]{1,0:T(8,128)(2,1)S(1)}, u32[]{:S(2)}, u32[]{:S(2)}) collective-permute-start(bf16[256,2048]{1,0:T(8,128)(2,1)S(1)} %broadcast_select_fusion), channel_id=1, source_target_pairs={{16,24},{17,25},{10,2},{11,3},{20,28},{21,29},{14,6},{15,7}} | collective-permute-start | bytes 3145736 | tf_op jit(solution)/shard_map/ppermute | solution.py:457
  80.0 2.6 %collective-permute-start.9 = (bf16[128,2048]{1,0:T(8,128)(2,1)S(1)}, bf16[128,2048]{1,0:T(8,128)(2,1)S(1)}, u32[]{:S(2)}, u32[]{:S(2)}) collective-permute-start(bf16[128,2048]{1,0:T(8,128)(2,1)S(1)} %collective-permute-done.5.refs_6_), channel_id=1, source_target_pairs={{0,1},{1,0},{2,3},{3,2},{4,5},{5,4},{6,7},{7,6},{8,9},{9,8},{10,11... | collective-permute-start | bytes 1572872 | tf_op jit(solution)/shard_map/ppermute | solution.py:462
  80.5 13.9 %collective-permute-start.11 = (bf16[128,2048]{1,0:T(8,128)(2,1)S(1)}, bf16[128,2048]{1,0:T(8,128)(2,1)S(1)}, u32[]{:S(2)}, u32[]{:S(2)}) collective-permute-start(bf16[128,2048]{1,0:T(8,128)(2,1)S(1)} %collective-permute-done.3.refs_2_), channel_id=1, source_target_pairs={{0,4},{1,5},{2,6},{3,7},{4,0},{5,1},{6,2},{7,3},{8,12},{9,13},{10,... | collective-permute-start | bytes 1572872 | tf_op jit(solution)/shard_map/ppermute | solution.py:462
  80.5 13.9 %collective-permute-start.13 = (bf16[128,2048]{1,0:T(8,128)(2,1)S(1)}, bf16[128,2048]{1,0:T(8,128)(2,1)S(1)}, u32[]{:S(2)}, u32[]{:S(2)}) collective-permute-start(bf16[128,2048]{1,0:T(8,128)(2,1)S(1)} %collective-permute-done.6.refs_8_), channel_id=1, source_target_pairs={{0,2},{1,3},{2,0},{3,1},{4,6},{5,7},{6,4},{7,5},{8,10},{9,11},{10,... | collective-permute-start | bytes 1572872 | tf_op jit(solution)/shard_map/ppermute | solution.py:462
  81.9 13.0 %collective-permute-start.7 = (bf16[128,2048]{1,0:T(8,128)(2,1)S(1)}, bf16[128,2048]{1,0:T(8,128)(2,1)S(1)}, u32[]{:S(2)}, u32[]{:S(2)}) collective-permute-start(bf16[128,2048]{1,0:T(8,128)(2,1)S(1)} %collective-permute-done.3.refs_2_), channel_id=1, source_target_pairs={{0,1},{1,0},{2,3},{3,2},{4,5},{5,4},{6,7},{7,6},{8,9},{9,8},{10,11... | collective-permute-start | bytes 1572872 | tf_op jit(solution)/shard_map/ppermute | solution.py:462
  82.6 12.3 %collective-permute-start.10 = (bf16[128,2048]{1,0:T(8,128)(2,1)S(1)}, bf16[128,2048]{1,0:T(8,128)(2,1)S(1)}, u32[]{:S(2)}, u32[]{:S(2)}) collective-permute-start(bf16[128,2048]{1,0:T(8,128)(2,1)S(1)} %collective-permute-done.6.refs_8_), channel_id=1, source_target_pairs={{0,1},{1,0},{2,3},{3,2},{4,5},{5,4},{6,7},{7,6},{8,9},{9,8},{10,11... | collective-permute-start | bytes 1572872 | tf_op jit(solution)/shard_map/ppermute | solution.py:462
  94.4 2.7 %collective-permute-start.14 = (bf16[128,2048]{1,0:T(8,128)(2,1)S(1)}, bf16[128,2048]{1,0:T(8,128)(2,1)S(1)}, u32[]{:S(2)}, u32[]{:S(2)}) collective-permute-start(bf16[128,2048]{1,0:T(8,128)(2,1)S(1)} %collective-permute-done.13.refs_12_), channel_id=1, source_target_pairs={{0,1},{1,0},{2,3},{3,2},{4,5},{5,4},{6,7},{7,6},{8,9},{9,8},{10,11... | collective-permute-start | bytes 1572872 | tf_op jit(solution)/shard_map/ppermute | solution.py:462
  105.5 21.2 %all-to-all-start.1 = ((bf16[8,256,256]{2,1,0:T(8,128)(2,1)}), bf16[8,256,256]{2,1,0:T(8,128)(2,1)S(1)}, u32[]{:S(2)}, u32[]{:S(2)}) async-start(bf16[8,256,256]{2,1,0:T(8,128)(2,1)} %get-tuple-element.84), calls=%async_computation.1 | async-start | bytes 2097152 | tf_op jit(solution)/shard_map/all_to_all | solution.py:441
  126.7 46.5 %all-to-all-start.2 = ((bf16[8,256,384]{2,1,0:T(8,128)(2,1)}), bf16[8,256,384]{2,1,0:T(8,128)(2,1)S(1)}, u32[]{:S(2)}, u32[]{:S(2)}) async-start(bf16[8,256,384]{2,1,0:T(8,128)(2,1)} %bitcast.32), calls=%async_computation.2 | async-start | bytes 3145728 | tf_op jit(solution)/shard_map/all_to_all | solution.py:441
  130.9 17.1 %collective-permute-start.16 = (bf16[512,256]{1,0:T(8,128)(2,1)S(1)}, bf16[512,256]{1,0:T(8,128)(2,1)S(1)}, u32[]{:S(2)}, u32[]{:S(2)}) collective-permute-start(bf16[512,256]{1,0:T(8,128)(2,1)S(1)} %get-tuple-element.90), channel_id=1, source_target_pairs={{0,8},{8,0},{16,24},{24,16},{1,9},{9,1},{17,25},{25,17},{2,10},{10... | collective-permute-start | bytes 786440 | tf_op jit(solution)/shard_map/ppermute | solution.py:594
  131.0 17.1 %collective-permute-start.17 = (bf16[512,256]{1,0:T(8,128)(2,1)S(1)}, bf16[512,256]{1,0:T(8,128)(2,1)S(1)}, u32[]{:S(2)}, u32[]{:S(2)}) collective-permute-start(bf16[512,256]{1,0:T(8,128)(2,1)S(1)} %get-tuple-element.91), channel_id=1, source_target_pairs={{0,16},{8,24},{16,0},{24,8},{1,17},{9,25},{17,1},{25,9},{2,18},{10... | collective-permute-start | bytes 786440 | tf_op jit(solution)/shard_map/ppermute | solution.py:594
  131.0 26.5 %collective-permute-start.18 = (bf16[512,256]{1,0:T(8,128)(2,1)S(1)}, bf16[512,256]{1,0:T(8,128)(2,1)S(1)}, u32[]{:S(2)}, u32[]{:S(2)}) collective-permute-start(bf16[512,256]{1,0:T(8,128)(2,1)S(1)} %get-tuple-element.92), channel_id=1, source_target_pairs={{0,24},{8,16},{16,8},{24,0},{1,25},{9,17},{17,9},{25,1},{2,26},{10... | collective-permute-start | bytes 786440 | tf_op jit(solution)/shard_map/ppermute | solution.py:594
  157.6 12.8 %collective-permute-start.21 = (bf16[512,256]{1,0:T(8,128)(2,1)S(1)}, bf16[512,256]{1,0:T(8,128)(2,1)S(1)}, u32[]{:S(2)}, u32[]{:S(2)}) collective-permute-start(bf16[512,256]{1,0:T(8,128)(2,1)S(1)} %add_convert_fusion.refs_0_), channel_id=1, source_target_pairs={{0,6},{1,7},{2,4},{3,5},{4,2},{5,3},{6,0},{7,1},{8,14},{9,15},{10,... | collective-permute-start | bytes 786440 | tf_op jit(solution)/shard_map/ppermute | solution.py:462
  160.3 12.2 %collective-permute-start.20 = (bf16[512,256]{1,0:T(8,128)(2,1)S(1)}, bf16[512,256]{1,0:T(8,128)(2,1)S(1)}, u32[]{:S(2)}, u32[]{:S(2)}) collective-permute-start(bf16[512,256]{1,0:T(8,128)(2,1)S(1)} %add_convert_fusion.refs_0_), channel_id=1, source_target_pairs={{0,4},{1,5},{2,6},{3,7},{4,0},{5,1},{6,2},{7,3},{8,12},{9,13},{10,... | collective-permute-start | bytes 786440 | tf_op jit(solution)/shard_map/ppermute | solution.py:462
  160.8 12.3 %collective-permute-start.19 = (bf16[512,256]{1,0:T(8,128)(2,1)S(1)}, bf16[512,256]{1,0:T(8,128)(2,1)S(1)}, u32[]{:S(2)}, u32[]{:S(2)}) collective-permute-start(bf16[512,256]{1,0:T(8,128)(2,1)S(1)} %add_convert_fusion.refs_0_), channel_id=1, source_target_pairs={{0,2},{1,3},{2,0},{3,1},{4,6},{5,7},{6,4},{7,5},{8,10},{9,11},{10,... | collective-permute-start | bytes 786440 | tf_op jit(solution)/shard_map/ppermute | solution.py:462
  173.9 24.5 %all-to-all-start.3 = ((bf16[8,256,384]{2,1,0:T(8,128)(2,1)}), bf16[8,256,384]{2,1,0:T(8,128)(2,1)S(1)}, u32[]{:S(2)}, u32[]{:S(2)}) async-start(bf16[8,256,384]{2,1,0:T(8,128)(2,1)} %bitcast.33), calls=%async_computation.3 | async-start | bytes 3145728 | tf_op jit(solution)/shard_map/all_to_all | solution.py:441
  (22 other events, 261.0 us)
where the time goes:
time: 201 us
  Pallas kernels  81.1 us (40%)
  waiting for transfers between devices  77.3 us (38%)
  starting transfers between devices  37.2 us (19%)
  local copies, waits for them, and re-layouts  3.17 us (2%)
    all_to_all x4, waiting for transfers between devices, exchange(): lax.all_to_all(chunks, 'seq', split_axis=0, concat_axis=0, tiled=True)  47.9 us
    pallas_call x3, Pallas kernels, backward(): pl.pallas_call(functools.partial(backward_kernel, blocks=blocks, begin=be...  40.3 us
    pallas_call x2, Pallas kernels, forward(): pl.pallas_call(functools.partial(forward_kernel, begin=begin, end=end), i...  21 us
    ppermute x20, waiting for transfers between devices, swap(): return lax.ppermute(array, 'seq', routes)  19.9 us
    all_to_all x4, starting transfers between devices, exchange(): lax.all_to_all(chunks, 'seq', split_axis=0, concat_axis=0, tiled=True)  15.3 us
    ppermute x20, starting transfers between devices, swap(): return lax.ppermute(array, 'seq', routes)  10.6 us
    ppermute x3, waiting for transfers between devices, pair_device(): lax.ppermute(parts[offset], 'fsdp', [(z, z ^ offset) for z in range(plane...  9.48 us
    ppermute x3, starting transfers between devices, send_weight(): return lax.ppermute(rows, ('fsdp', 'seq'), routes)  7.74 us
  transfers between devices with their start and end apart: 30, of which 13 were waited for; matrix products, arithmetic and copies ran while one was open for 1% of the time, Pallas kernels for 33%

commit v1 on v0

--- a/solution.py
+++ b/solution.py
@@ -175,7 +175,7 @@
 
 
 def forward_kernel(adjacency, counts, packed, *refs, begin, end):
-    carried, (first, second, stats, value_t) = refs[:-4], refs[-4:]
+    carried, (first, second, stats, value_t, queries_t, turned) = refs[:-6], refs[-6:]
     outs = (first, second)
     blocks = packed.shape[0] // BLK
     if begin:
@@ -183,18 +183,22 @@
         first[done, :], second[done, :] = carried[0][done, :], carried[1][done, :]
         stats[:, : 8 * begin, :] = carried[2][:, : 8 * begin, :]
 
-    @pl.loop(0, blocks)
+    @pl.loop(0, blocks, unroll=4)
     def _(index):
         for pair in range(2):
             value_t[pair, index] = packed[block_rows(index), columns(pair, 2)].T
+
+    @pl.loop(begin, end, unroll=4)
+    def _(index):
+        for pair in range(2):
+            queries_t[pair, index - begin] = by_head_t(packed[block_rows(index), columns(pair, 0)])
 
     def query_block(index, slots):
         picked = [adjacency[index, slot] for slot in range(slots)]
         places = [block_rows(block) for block in picked]
         raws = []
         for pair in range(2):
-            queries = by_head_t(packed[block_rows(index), columns(pair, 0)])
-            raw = stack(packed.at[:, columns(pair, 1)], places, queries)
+            raw = stack(packed.at[:, columns(pair, 1)], places, queries_t[pair, index - begin])
             unsure = jnp.where(slots - 1 < counts[index], raw[-BLK:], NEG_FILL)
             raws.append(jnp.concatenate([raw[:-BLK], unsure], axis=0))
         for pair, raw in enumerate(raws):
@@ -205,12 +209,18 @@
                 jnp.concatenate([value_t[pair, block] for block in picked], axis=1),
                 expo.astype(jnp.bfloat16),
             )
-            outs[pair][block_rows(index), :] = own_parts(out_t / row_sum).T.astype(jnp.bfloat16)
+            turned[pair, index - begin] = out_t / row_sum
             stats[pair, block_rows(index, 8), :] = jnp.broadcast_to(
                 row_max * BASE2 + jnp.log2(row_sum), (8, 2 * BLK)
             )
 
     each_block(counts, begin, end, 2, query_block)
+
+    @pl.loop(begin, end, unroll=4)
+    def _(index):
+        for pair in range(2):
+            out_t = own_parts(turned[pair, index - begin])
+            outs[pair][block_rows(index), :] = out_t.T.astype(jnp.bfloat16)
 
 
 def backward_kernel(
@@ -218,10 +228,10 @@
 ):
     query, key, value = (packed.at[:, pl.ds(PAIR * part, PAIR)] for part in range(3))
     carried, rest = refs[: 3 if begin else 0], refs[3 if begin else 0 :]
-    outs, (key_t, key_sum, value_sum) = rest[:-3], rest[-3:]
+    outs, (key_t, key_sum, value_sum, queries_t, grads_t, row_dot, turned) = rest[:-7], rest[-7:]
     query_g = outs[0]
 
-    @pl.loop(0, blocks)
+    @pl.loop(0, blocks, unroll=4)
     def _(index):
         key_t[index] = key[block_rows(index), :].T
         if begin:
@@ -231,35 +241,49 @@
             key_sum[block_rows(index), :] = jnp.zeros((BLK, PAIR), jnp.float32)
             value_sum[block_rows(index), :] = jnp.zeros((BLK, PAIR), jnp.float32)
 
-    def query_block(index, slots):
-        picked = [adjacency[index, slot] for slot in range(slots)]
-        query_rows = query[block_rows(index), :]
+    @pl.loop(begin, end, unroll=(end - begin) % 4 == 0 and 4 or end - begin)
+    def _(index):
         grad_rows = grad[block_rows(index), :]
-        queries, queries_t = by_head(query_rows), by_head_t(query_rows)
-        grads, grads_t = by_head(grad_rows), by_head_t(grad_rows)
-        stat = stats[0, pl.ds(pl.multiple_of(index * 8, 8), 1), :]
+        queries_t[index - begin] = by_head_t(query[block_rows(index), :])
+        grads_t[index - begin] = by_head_t(grad_rows)
         products = (
             grad_rows.astype(jnp.float32) * attn_out[block_rows(index), :].astype(jnp.float32)
         ).T
-        row_dot = jnp.concatenate(
-            [
-                jnp.sum(products[:HD], axis=0, keepdims=True),
-                jnp.sum(products[HD:], axis=0, keepdims=True),
-            ],
-            axis=1,
-        )
+        row_dot[block_rows(index - begin, 8), :] = jnp.broadcast_to(
+            jnp.concatenate(
+                [
+                    jnp.sum(products[:HD], axis=0, keepdims=True),
+                    jnp.sum(products[HD:], axis=0, keepdims=True),
+                ],
+                axis=1,
+            ),
+            (8, 2 * BLK),
+        )
+
+    def query_block(index, slots):
+        picked = [adjacency[index, slot] for slot in range(slots)]
         places = [block_rows(block) for block in picked]
-        prob = jnp.exp2(stack(key, places, queries_t) * BASE2 - stat)
-        term = (prob * (stack(value, places, grads_t) - row_dot)).astype(jnp.bfloat16)
+        queries, grads = by_head(query[block_rows(index), :]), by_head(grad[block_rows(index), :])
+        stat = stats[0, pl.ds(pl.multiple_of(index * 8, 8), 1), :]
+        prob = jnp.exp2(stack(key, places, queries_t[index - begin]) * BASE2 - stat)
+        change = stack(value, places, grads_t[index - begin])
+        change = change - row_dot[pl.ds(pl.multiple_of((index - begin) * 8, 8), 1), :]
+        term = (prob * change).astype(jnp.bfloat16)
         key_terms = dot(term, queries)
         value_terms = dot(prob.astype(jnp.bfloat16), grads)
         for number, at in enumerate(places):
             key_sum[at, :] += key_terms[BLK * number : BLK * (number + 1)]
             value_sum[at, :] += value_terms[BLK * number : BLK * (number + 1)]
-        query_t = dot(jnp.concatenate([key_t[block] for block in picked], axis=1), term)
-        query_g[block_rows(index), :PAIR] = (own_parts(query_t).T * SCALE).astype(jnp.bfloat16)
+        turned[index - begin] = dot(jnp.concatenate([key_t[block] for block in picked], axis=1), term)
 
     each_block(counts, begin, end, 1, query_block)
+
+    @pl.loop(begin, end, unroll=(end - begin) % 4 == 0 and 4 or end - begin)
+    def _(index):
+        query_g[block_rows(index), :PAIR] = (
+            own_parts(turned[index - begin]).T * SCALE
+        ).astype(jnp.bfloat16)
+
     if end < blocks:
         outs[1][...], outs[2][...] = key_sum[...], value_sum[...]
     else:
@@ -297,7 +321,11 @@
             jax.ShapeDtypeStruct((tokens, PAIR), jnp.bfloat16),
             jax.ShapeDtypeStruct((2, blocks * 8, 2 * BLK), jnp.float32),
         ],
-        scratch_shapes=[pltpu.VMEM((2, blocks, PAIR, BLK), jnp.bfloat16)],
+        scratch_shapes=[
+            pltpu.VMEM((2, blocks, PAIR, BLK), jnp.bfloat16),
+            pltpu.VMEM((2, end - begin, PAIR, 2 * BLK), jnp.bfloat16),
+            pltpu.VMEM((2, end - begin, PAIR, 2 * BLK), jnp.float32),
+        ],
         compiler_params=PARAMS,
         cost_estimate=cost(tokens * (end - begin) // blocks, 4),
         name="attend_forward",
@@ -331,6 +359,10 @@
             pltpu.VMEM((blocks, PAIR, BLK), jnp.bfloat16),
             pltpu.VMEM((tokens, PAIR), jnp.float32),
             pltpu.VMEM((tokens, PAIR), jnp.float32),
+            pltpu.VMEM((end - begin, PAIR, 2 * BLK), jnp.bfloat16),
+            pltpu.VMEM((end - begin, PAIR, 2 * BLK), jnp.bfloat16),
+            pltpu.VMEM(((end - begin) * 8, 2 * BLK), jnp.float32),
+            pltpu.VMEM((end - begin, PAIR, 2 * BLK), jnp.float32),
         ],
         compiler_params=WIDE,
         cost_estimate=cost(tokens * (end - begin) // blocks, 5),
@@ -464,8 +496,8 @@
 
 def project_kernel(places, *refs):
     pieces, rest = refs[: len(places)], refs[len(places) :]
-    weights, (first, second, attn_grad, terms) = rest[:4], rest[4:8]
-    whole, weight, weight_t, landed, fetched = rest[8:]
+    weights, (first, second, given, sent) = rest[:4], rest[4:8]
+    whole, weight, weight_t, attn_grad, terms, landed, fetched, left, gone = rest[8:]
     plane, member = lax.axis_index("fsdp"), lax.axis_index("seq")
     local = whole.shape[0] // terms.shape[0]
     copies = []
@@ -493,10 +525,19 @@
         wide = dot(attn_t, whole[:, width * group : width * (group + 2)]).astype(terms.dtype)
         terms[group], terms[group + 1] = wide[:, :width], wide[:, width:]
 
+    leaving = pltpu.make_async_copy(terms, sent, left)
+    leaving.start()
+
     @pl.loop(0, 4)
     def _(part):
         rows = block_rows(part, whole.shape[0] // 4)
         attn_grad[rows, :] = dot(whole[rows, :], weight_t[...]).astype(attn_grad.dtype)
+        pltpu.make_async_copy(attn_grad.at[rows, :], given.at[rows, :], gone.at[part]).start()
+
+    leaving.wait()
+    for part in range(4):
+        rows = block_rows(part, whole.shape[0] // 4)
+        pltpu.make_async_copy(attn_grad.at[rows, :], given.at[rows, :], gone.at[part]).wait()
 
 
 def project(pieces, weights, first, second, groups):
@@ -508,7 +549,7 @@
     return pl.pallas_call(
         functools.partial(project_kernel, places),
         in_specs=[far] * (len(arrays) + len(weights)) + [VMEM] * 2,
-        out_specs=[VMEM] * 2,
+        out_specs=[pl.BlockSpec(memory_space=pltpu.HBM)] * 2,
         out_shape=[
             jax.ShapeDtypeStruct((tokens, height), jnp.bfloat16),
             jax.ShapeDtypeStruct((groups, height, width // groups), jnp.bfloat16),
@@ -517,8 +558,12 @@
             pltpu.VMEM((tokens, width), jnp.bfloat16),
             pltpu.VMEM((height, width), jnp.bfloat16),
             pltpu.VMEM((width, height), jnp.bfloat16),
+            pltpu.VMEM((tokens, height), jnp.bfloat16),
+            pltpu.VMEM((groups, height, width // groups), jnp.bfloat16),
             pltpu.SemaphoreType.DMA((len(arrays),)),
             pltpu.SemaphoreType.DMA,
+            pltpu.SemaphoreType.DMA,
+            pltpu.SemaphoreType.DMA((4,)),
         ],
         compiler_params=PARAMS,
         cost_estimate=pl.CostEstimate(
@@ -595,7 +640,7 @@
         for offset in range(1, planes)
     ]
     first_r = exchange(first_g.reshape(members, local_tokens, 3 * PAIR))
-    split_at = tokens // BLK * 11 // 16
+    split_at = tokens // BLK * 12 // 16
     started = backward(
         packed, attn_grad, 1, second, stats, adjacency, counts, end=split_at
     )

time: 201 us -> 198 us (0.985)
  starting transfers between devices: 37.2 us -> 34.2 us
    ppermute x3, starting transfers between devices: 7.74 us -> 4.41 us  [send_weight(): return lax.ppermute(rows, ('fsdp', 'seq'), routes)]
where the time goes in v1:
time: 198 us; the launch traced here: 197 us
  Pallas kernels  80 us (40%)
  waiting for transfers between devices  77.3 us (39%)
  starting transfers between devices  34.2 us (17%)
  local copies, waits for them, and re-layouts  3.17 us (2%)
    all_to_all x4, waiting for transfers between devices, exchange(): lax.all_to_all(chunks, 'seq', split_axis=0, concat_axis=0, tiled=True)  47.9 us
    pallas_call x3, Pallas kernels, backward(): pl.pallas_call(functools.partial(backward_kernel, blocks=blocks, begin=be...  39.4 us
    pallas_call x2, Pallas kernels, forward(): pl.pallas_call(functools.partial(forward_kernel, begin=begin, end=end), i...  21 us
    ppermute x20, waiting for transfers between devices, swap(): return lax.ppermute(array, 'seq', routes)  20 us
    all_to_all x4, starting transfers between devices, exchange(): lax.all_to_all(chunks, 'seq', split_axis=0, concat_axis=0, tiled=True)  15.1 us
    ppermute x20, starting transfers between devices, swap(): return lax.ppermute(array, 'seq', routes)  11.1 us
    ppermute x3, waiting for transfers between devices, pair_device(): lax.ppermute(parts[offset], 'fsdp', [(z, z ^ offset) for z in range(plane...  9.32 us
    pallas_call x1, Pallas kernels, project(): pl.pallas_call(functools.partial(project_kernel, places), in_specs=[far]...  7.28 us
  transfers between devices with their start and end apart: 30, of which 13 were waited for; matrix products, arithmetic and copies ran while one was open for 1% of the time, Pallas kernels for 33%

profile of v1, /device:TPU:16, one launch (start us, length us, event | category | flops | bytes accessed | tf_op | source)
XLA Modules:
  0.0 197.0 jit_solution(4874732854504057117)
XLA Ops:
  0.6 5.4 %pack.1 = (bf16[8,256,768]{2,1,0:T(8,128)(2,1)}, bf16[128,2048]{1,0:T(8,128)(2,1)}, bf16[128,2048]{1,0:T(8,128)(2,1)}, bf16[256,2048]{1,0:T(8,128)(2,1)}) custom-call(bf16[256,2048]{1,0:T(8,128)(2,1)} %bitcast.34, bf16[256,2048]{1,0:T(8,128)(2,1)} %bitcast.35, bf16[256,2048]{1,0:T(8,128)(2,1)} %bitcast.36, bf16[256,2048]{1,0:T(8,128)(2,1)} %bitcast.19, ...), custom_call_target="tpu_custom_call" | custom-call | tf_op jit(solution)/shard_map/pack/pallas_call | solution.py:404
  6.0 3.9 %all-to-all-start = ((bf16[8,256,768]{2,1,0:T(8,128)(2,1)}), bf16[8,256,768]{2,1,0:T(8,128)(2,1)S(1)}, u32[]{:S(2)}, u32[]{:S(2)}) async-start(bf16[8,256,768]{2,1,0:T(8,128)(2,1)} %get-tuple-element.56), calls=%async_computation | async-start | bytes 6291456 | tf_op jit(solution)/shard_map/all_to_all | solution.py:473
  10.4 1.6 collective-permute-start
  13.5 34.3 %all-to-all-done = bf16[8,256,768]{2,1,0:T(8,128)(2,1)S(1)} async-done(((bf16[8,256,768]{2,1,0:T(8,128)(2,1)}), bf16[8,256,768]{2,1,0:T(8,128)(2,1)S(1)}, u32[]{:S(2)}, u32[]{:S(2)}) %all-to-all-start) | async-done | bytes 3145760 | tf_op jit(solution)/shard_map/all_to_all | solution.py:473
  50.3 1.5 collective-permute-start.4
  51.9 10.4 %attend_forward.2 = (bf16[2048,128]{1,0:T(8,128)(2,1)S(1)}, bf16[2048,128]{1,0:T(8,128)(2,1)S(1)}, f32[2,128,256]{2,1,0:T(8,128)S(1)}) custom-call(s32[16,10]{1,0:T(8,128)S(1)} %bitcast.22, s32[16]{0:T(128)S(1)} %bitcast.30, bf16[2048,768]{1,0:T(8,128)(2,1)S(1)} %bitcast.14), custom_call_target="tpu_custom_call" | custom-call | flops 5368709120 | bytes 1572864 | tf_op jit(solution)/shard_map/attend_forward/pallas_call | solution.py:315
  63.6 1.5 collective-permute-start.15
  65.1 10.7 %attend_forward.3 = (bf16[2048,128]{1,0:T(8,128)(2,1)S(1)}, bf16[2048,128]{1,0:T(8,128)(2,1)S(1)}, f32[2,128,256]{2,1,0:T(8,128)S(1)}) custom-call(s32[16,10]{1,0:T(8,128)S(1)} %bitcast.23, s32[16]{0:T(128)S(1)} %bitcast.31, bf16[2048,768]{1,0:T(8,128)(2,1)S(1)} %bitcast.15, bf16[2048,128]{1,0:T(8,128)(2,1)S(1)} %get-tuple-element.66.refs_0_, ...), custom_call_target="tpu_custom_call" | custom-call | flops 5368709120 | bytes 1572864 | tf_op jit(solution)/shard_map/attend_forward/pallas_call | solution.py:315
  79.4 11.6 %collective-permute-done.11.refs_10_ = bf16[128,2048]{1,0:T(8,128)(2,1)S(1)} collective-permute-done((bf16[128,2048]{1,0:T(8,128)(2,1)S(1)}, bf16[128,2048]{1,0:T(8,128)(2,1)S(1)}, u32[]{:S(2)}, u32[]{:S(2)}) %collective-permute-start.11) | collective-permute-done | bytes 524320 | tf_op jit(solution)/shard_map/ppermute | solution.py:494
  91.5 1.4 collective-permute-done.12.refs_11_
  93.7 7.3 %project.1 = (bf16[2048,256]{1,0:T(8,128)(2,1)S(1)}, bf16[8,256,256]{2,1,0:T(8,128)(2,1)}) custom-call(bf16[256,2048]{1,0:T(8,128)(2,1)S(1)} %bitcast.21, bf16[256,2048]{1,0:T(8,128)(2,1)} %collective-permute-done.1.refs_1_, bf16[128,2048]{1,0:T(8,128)(2,1)S(1)} %collective-permute-done.3.refs_2_, bf16[128,2048]{1,0:T(8,128)(2,1)S(1)} %collective-permute-done.7.refs_3_, ...), custom_call_target="tpu_custom_call" | custom-call | flops 4294967296 | bytes 12582912 | tf_op jit(solution)/shard_map/project/pallas_call | solution.py:549
  102.0 3.6 %all-to-all-start.1 = ((bf16[8,256,256]{2,1,0:T(8,128)(2,1)}), bf16[8,256,256]{2,1,0:T(8,128)(2,1)S(1)}, u32[]{:S(2)}, u32[]{:S(2)}) async-start(bf16[8,256,256]{2,1,0:T(8,128)(2,1)} %get-tuple-element.84), calls=%async_computation.1 | async-start | bytes 2097152 | tf_op jit(solution)/shard_map/all_to_all | solution.py:473
  105.5 17.4 %attend_backward.3 = bf16[2048,384]{1,0:T(8,128)(2,1)} custom-call(s32[16,10]{1,0:T(8,128)} %bitcast.24, s32[16]{0:T(128)} %bitcast.27, bf16[2048,768]{1,0:T(8,128)(2,1)} %bitcast.16, bf16[2048,256]{1,0:T(8,128)(2,1)} %copy-done.5, bf16[2048,128]{1,0:T(8,128)(2,1)} %copy-done.7, f32[2,128,256]{2,1,0:T(8,128)} %copy-done.8), custom_call_target="tpu_custom_call" | custom-call | flops 13421772800 | bytes 3145728 | tf_op jit(solution)/shard_map/attend_backward/pallas_call | solution.py:349
  123.0 4.1 %all-to-all-start.2 = ((bf16[8,256,384]{2,1,0:T(8,128)(2,1)}), bf16[8,256,384]{2,1,0:T(8,128)(2,1)S(1)}, u32[]{:S(2)}, u32[]{:S(2)}) async-start(bf16[8,256,384]{2,1,0:T(8,128)(2,1)} %bitcast.32), calls=%async_computation.2 | async-start | bytes 3145728 | tf_op jit(solution)/shard_map/all_to_all | solution.py:473
  127.6 3.1 %collective-permute-start.18 = (bf16[512,256]{1,0:T(8,128)(2,1)S(1)}, bf16[512,256]{1,0:T(8,128)(2,1)S(1)}, u32[]{:S(2)}, u32[]{:S(2)}) collective-permute-start(bf16[512,256]{1,0:T(8,128)(2,1)S(1)} %get-tuple-element.92), channel_id=1, source_target_pairs={{0,24},{8,16},{16,8},{24,0},{1,25},{9,17},{17,9},{25,1},{2,26},{10... | collective-permute-start | bytes 786440 | tf_op jit(solution)/shard_map/ppermute | solution.py:639
  130.7 14.0 %attend_backward.4 = (bf16[2048,128]{1,0:T(8,128)(2,1)}, f32[2048,128]{1,0:T(8,128)}, f32[2048,128]{1,0:T(8,128)}) custom-call(s32[16,10]{1,0:T(8,128)} %bitcast.25, s32[16]{0:T(128)} %bitcast.28, bf16[2048,768]{1,0:T(8,128)(2,1)} %bitcast.17, bf16[2048,256]{1,0:T(8,128)(2,1)} %copy-done.5, bf16[2048,128]{1,0:T(8,128)(2,1)} %copy-done.6, ...), custom_call_target="tpu_custom_call" | custom-call | flops 10066329600 | bytes 2359296 | tf_op jit(solution)/shard_map/attend_backward/pallas_call | solution.py:349
  144.7 9.3 %collective-permute-done.18 = bf16[512,256]{1,0:T(8,128)(2,1)S(1)} collective-permute-done((bf16[512,256]{1,0:T(8,128)(2,1)S(1)}, bf16[512,256]{1,0:T(8,128)(2,1)S(1)}, u32[]{:S(2)}, u32[]{:S(2)}) %collective-permute-start.18) | collective-permute-done | bytes 262176 | tf_op jit(solution)/shard_map/ppermute | solution.py:639
  154.2 2.6 %collective-permute-start.21 = (bf16[512,256]{1,0:T(8,128)(2,1)S(1)}, bf16[512,256]{1,0:T(8,128)(2,1)S(1)}, u32[]{:S(2)}, u32[]{:S(2)}) collective-permute-start(bf16[512,256]{1,0:T(8,128)(2,1)S(1)} %add_convert_fusion.refs_0_), channel_id=1, source_target_pairs={{0,6},{1,7},{2,4},{3,5},{4,2},{5,3},{6,0},{7,1},{8,14},{9,15},{10,... | collective-permute-start | bytes 786440 | tf_op jit(solution)/shard_map/ppermute | solution.py:494
  157.7 8.0 %attend_backward.5 = bf16[2048,384]{1,0:T(8,128)(2,1)} custom-call(s32[16,10]{1,0:T(8,128)} %bitcast.26, s32[16]{0:T(128)} %bitcast.29, bf16[2048,768]{1,0:T(8,128)(2,1)} %bitcast.18, bf16[2048,256]{1,0:T(8,128)(2,1)} %copy-done.5, bf16[2048,128]{1,0:T(8,128)(2,1)} %copy-done.6, f32[2,128,256]{2,1,0:T(8,128)} %copy-done.8, ...), custom_call_target="tpu_custom_call" | custom-call | flops 3355443200 | bytes 786432 | tf_op jit(solution)/shard_map/attend_backward/pallas_call | solution.py:349
  165.7 2.7 %collective-permute-done.20.refs_4_ = bf16[512,256]{1,0:T(8,128)(2,1)S(1)} collective-permute-done((bf16[512,256]{1,0:T(8,128)(2,1)S(1)}, bf16[512,256]{1,0:T(8,128)(2,1)S(1)}, u32[]{:S(2)}, u32[]{:S(2)}) %collective-permute-start.20) | collective-permute-done | bytes 262176 | tf_op jit(solution)/shard_map/ppermute | solution.py:494
  169.8 3.6 %all-to-all-start.3 = ((bf16[8,256,384]{2,1,0:T(8,128)(2,1)}), bf16[8,256,384]{2,1,0:T(8,128)(2,1)S(1)}, u32[]{:S(2)}, u32[]{:S(2)}) async-start(bf16[8,256,384]{2,1,0:T(8,128)(2,1)} %bitcast.33), calls=%async_computation.3 | async-start | bytes 3145728 | tf_op jit(solution)/shard_map/all_to_all | solution.py:473
  176.5 4.2 %spread.1 = f32[512,2048]{1,0:T(8,128)} custom-call(bf16[512,256]{1,0:T(8,128)(2,1)} %copy-done.9, bf16[512,256]{1,0:T(8,128)(2,1)} %copy-done.13, bf16[512,256]{1,0:T(8,128)(2,1)} %copy-done.12, bf16[512,256]{1,0:T(8,128)(2,1)} %copy-done.14, bf16[512,256]{1,0:T(8,128)(2,1)} %copy-done.11, bf16[512,256]{1,0:T(8,128)(2,1)} %collective-permute-done.24.refs_5_, ...), custom_call_target="tpu_custom_call" | custom-call | tf_op jit(solution)/shard_map/spread/pallas_call | solution.py:461
  180.7 13.6 %all-to-all-done.3.second = bf16[8,256,384]{2,1,0:T(8,128)(2,1)S(1)} async-done(((bf16[8,256,384]{2,1,0:T(8,128)(2,1)}), bf16[8,256,384]{2,1,0:T(8,128)(2,1)S(1)}, u32[]{:S(2)}, u32[]{:S(2)}) %all-to-all-start.3) | async-done | bytes 1572896 | tf_op jit(solution)/shard_map/all_to_all | solution.py:473
  194.3 2.7 %unpack.1 = (bf16[256,2048]{1,0:T(8,128)(2,1)}, bf16[256,2048]{1,0:T(8,128)(2,1)}, bf16[256,2048]{1,0:T(8,128)(2,1)}) custom-call(bf16[8,256,384]{2,1,0:T(8,128)(2,1)S(1)} %all-to-all-done.2.first, bf16[8,256,384]{2,1,0:T(8,128)(2,1)S(1)} %all-to-all-done.3.second), custom_call_target="tpu_custom_call" | custom-call | tf_op jit(solution)/shard_map/unpack/pallas_call | solution.py:438
  (81 shorter events, 17.7 us)
Async XLA Ops:
  6.0 41.8 %all-to-all-start = ((bf16[8,256,768]{2,1,0:T(8,128)(2,1)}), bf16[8,256,768]{2,1,0:T(8,128)(2,1)S(1)}, u32[]{:S(2)}, u32[]{:S(2)}) async-start(bf16[8,256,768]{2,1,0:T(8,128)(2,1)} %get-tuple-element.56), calls=%async_computation | async-start | bytes 6291456 | tf_op jit(solution)/shard_map/all_to_all | solution.py:473
  9.9 3.6 %collective-permute-start.1 = (bf16[256,2048]{1,0:T(8,128)(2,1)}, bf16[256,2048]{1,0:T(8,128)(2,1)}, u32[]{:S(2)}, u32[]{:S(2)}) collective-permute-start(bf16[256,2048]{1,0:T(8,128)(2,1)} %bitcast.20), channel_id=1, source_target_pairs={{0,1},{1,0},{2,3},{3,2},{4,5},{5,4},{6,7},{7,6},{8,9},{9,8},{10,11... | collective-permute-start | bytes 3145736 | tf_op jit(solution)/shard_map/ppermute | solution.py:494
  10.4 3.1 %collective-permute-start = (bf16[256,2048]{1,0:T(8,128)(2,1)}, bf16[256,2048]{1,0:T(8,128)(2,1)}, u32[]{:S(2)}, u32[]{:S(2)}) collective-permute-start(bf16[256,2048]{1,0:T(8,128)(2,1)} %get-tuple-element.59.refs_14_), channel_id=1, source_target_pairs={{0,8},{1,9},{10,18},{11,19},{20,12},{21,13},{30,22},{31,23}} | collective-permute-start | bytes 3145736 | tf_op jit(solution)/shard_map/ppermute | solution.py:489
  12.0 50.2 %collective-permute-start.2 = (bf16[256,2048]{1,0:T(8,128)(2,1)}, bf16[256,2048]{1,0:T(8,128)(2,1)}, u32[]{:S(2)}, u32[]{:S(2)}) collective-permute-start(bf16[256,2048]{1,0:T(8,128)(2,1)} %get-tuple-element.59.refs_14_), channel_id=1, source_target_pairs={{0,16},{1,17},{10,26},{11,27},{20,4},{21,5},{30,14},{31,15}} | collective-permute-start | bytes 3145736 | tf_op jit(solution)/shard_map/ppermute | solution.py:489
  47.8 28.7 %collective-permute-start.5 = (bf16[128,2048]{1,0:T(8,128)(2,1)}, bf16[128,2048]{1,0:T(8,128)(2,1)S(1)}, u32[]{:S(2)}, u32[]{:S(2)}) collective-permute-start(bf16[128,2048]{1,0:T(8,128)(2,1)} %get-tuple-element.72), channel_id=1, source_target_pairs={{0,4},{1,5},{2,6},{3,7},{4,0},{5,1},{6,2},{7,3},{8,12},{9,13},{10,... | collective-permute-start | bytes 1572872 | tf_op jit(solution)/shard_map/ppermute | solution.py:494
  48.3 28.2 %collective-permute-start.3 = (bf16[128,2048]{1,0:T(8,128)(2,1)}, bf16[128,2048]{1,0:T(8,128)(2,1)S(1)}, u32[]{:S(2)}, u32[]{:S(2)}) collective-permute-start(bf16[128,2048]{1,0:T(8,128)(2,1)} %get-tuple-element.72), channel_id=1, source_target_pairs={{0,2},{1,3},{2,0},{3,1},{4,6},{5,7},{6,4},{7,5},{8,10},{9,11},{10,... | collective-permute-start | bytes 1572872 | tf_op jit(solution)/shard_map/ppermute | solution.py:494
  48.9 27.6 %collective-permute-start.6 = (bf16[128,2048]{1,0:T(8,128)(2,1)}, bf16[128,2048]{1,0:T(8,128)(2,1)S(1)}, u32[]{:S(2)}, u32[]{:S(2)}) collective-permute-start(bf16[128,2048]{1,0:T(8,128)(2,1)} %get-tuple-element.73), channel_id=1, source_target_pairs={{0,4},{1,5},{2,6},{3,7},{4,0},{5,1},{6,2},{7,3},{8,12},{9,13},{10,... | collective-permute-start | bytes 1572872 | tf_op jit(solution)/shard_map/ppermute | solution.py:494
  50.3 26.2 %collective-permute-start.4 = (bf16[128,2048]{1,0:T(8,128)(2,1)}, bf16[128,2048]{1,0:T(8,128)(2,1)S(1)}, u32[]{:S(2)}, u32[]{:S(2)}) collective-permute-start(bf16[128,2048]{1,0:T(8,128)(2,1)} %get-tuple-element.73), channel_id=1, source_target_pairs={{0,2},{1,3},{2,0},{3,1},{4,6},{5,7},{6,4},{7,5},{8,10},{9,11},{10,... | collective-permute-start | bytes 1572872 | tf_op jit(solution)/shard_map/ppermute | solution.py:494
  63.6 27.9 %collective-permute-start.15 = (bf16[256,2048]{1,0:T(8,128)(2,1)S(1)}, bf16[256,2048]{1,0:T(8,128)(2,1)S(1)}, u32[]{:S(2)}, u32[]{:S(2)}) collective-permute-start(bf16[256,2048]{1,0:T(8,128)(2,1)S(1)} %broadcast_select_fusion), channel_id=1, source_target_pairs={{16,24},{17,25},{10,2},{11,3},{20,28},{21,29},{14,6},{15,7}} | collective-permute-start | bytes 3145736 | tf_op jit(solution)/shard_map/ppermute | solution.py:489
  76.6 2.6 %collective-permute-start.9 = (bf16[128,2048]{1,0:T(8,128)(2,1)S(1)}, bf16[128,2048]{1,0:T(8,128)(2,1)S(1)}, u32[]{:S(2)}, u32[]{:S(2)}) collective-permute-start(bf16[128,2048]{1,0:T(8,128)(2,1)S(1)} %collective-permute-done.5.refs_6_), channel_id=1, source_target_pairs={{0,1},{1,0},{2,3},{3,2},{4,5},{5,4},{6,7},{7,6},{8,9},{9,8},{10,11... | collective-permute-start | bytes 1572872 | tf_op jit(solution)/shard_map/ppermute | solution.py:494
  77.1 13.9 %collective-permute-start.11 = (bf16[128,2048]{1,0:T(8,128)(2,1)S(1)}, bf16[128,2048]{1,0:T(8,128)(2,1)S(1)}, u32[]{:S(2)}, u32[]{:S(2)}) collective-permute-start(bf16[128,2048]{1,0:T(8,128)(2,1)S(1)} %collective-permute-done.3.refs_2_), channel_id=1, source_target_pairs={{0,4},{1,5},{2,6},{3,7},{4,0},{5,1},{6,2},{7,3},{8,12},{9,13},{10,... | collective-permute-start | bytes 1572872 | tf_op jit(solution)/shard_map/ppermute | solution.py:494
  77.1 13.9 %collective-permute-start.13 = (bf16[128,2048]{1,0:T(8,128)(2,1)S(1)}, bf16[128,2048]{1,0:T(8,128)(2,1)S(1)}, u32[]{:S(2)}, u32[]{:S(2)}) collective-permute-start(bf16[128,2048]{1,0:T(8,128)(2,1)S(1)} %collective-permute-done.6.refs_8_), channel_id=1, source_target_pairs={{0,2},{1,3},{2,0},{3,1},{4,6},{5,7},{6,4},{7,5},{8,10},{9,11},{10,... | collective-permute-start | bytes 1572872 | tf_op jit(solution)/shard_map/ppermute | solution.py:494
  78.5 13.0 %collective-permute-start.7 = (bf16[128,2048]{1,0:T(8,128)(2,1)S(1)}, bf16[128,2048]{1,0:T(8,128)(2,1)S(1)}, u32[]{:S(2)}, u32[]{:S(2)}) collective-permute-start(bf16[128,2048]{1,0:T(8,128)(2,1)S(1)} %collective-permute-done.3.refs_2_), channel_id=1, source_target_pairs={{0,1},{1,0},{2,3},{3,2},{4,5},{5,4},{6,7},{7,6},{8,9},{9,8},{10,11... | collective-permute-start | bytes 1572872 | tf_op jit(solution)/shard_map/ppermute | solution.py:494
  79.3 12.3 %collective-permute-start.10 = (bf16[128,2048]{1,0:T(8,128)(2,1)S(1)}, bf16[128,2048]{1,0:T(8,128)(2,1)S(1)}, u32[]{:S(2)}, u32[]{:S(2)}) collective-permute-start(bf16[128,2048]{1,0:T(8,128)(2,1)S(1)} %collective-permute-done.6.refs_8_), channel_id=1, source_target_pairs={{0,1},{1,0},{2,3},{3,2},{4,5},{5,4},{6,7},{7,6},{8,9},{9,8},{10,11... | collective-permute-start | bytes 1572872 | tf_op jit(solution)/shard_map/ppermute | solution.py:494
  91.0 2.7 %collective-permute-start.14 = (bf16[128,2048]{1,0:T(8,128)(2,1)S(1)}, bf16[128,2048]{1,0:T(8,128)(2,1)S(1)}, u32[]{:S(2)}, u32[]{:S(2)}) collective-permute-start(bf16[128,2048]{1,0:T(8,128)(2,1)S(1)} %collective-permute-done.13.refs_12_), channel_id=1, source_target_pairs={{0,1},{1,0},{2,3},{3,2},{4,5},{5,4},{6,7},{7,6},{8,9},{9,8},{10,11... | collective-permute-start | bytes 1572872 | tf_op jit(solution)/shard_map/ppermute | solution.py:494
  102.0 21.0 %all-to-all-start.1 = ((bf16[8,256,256]{2,1,0:T(8,128)(2,1)}), bf16[8,256,256]{2,1,0:T(8,128)(2,1)S(1)}, u32[]{:S(2)}, u32[]{:S(2)}) async-start(bf16[8,256,256]{2,1,0:T(8,128)(2,1)} %get-tuple-element.84), calls=%async_computation.1 | async-start | bytes 2097152 | tf_op jit(solution)/shard_map/all_to_all | solution.py:473
  123.0 46.1 %all-to-all-start.2 = ((bf16[8,256,384]{2,1,0:T(8,128)(2,1)}), bf16[8,256,384]{2,1,0:T(8,128)(2,1)S(1)}, u32[]{:S(2)}, u32[]{:S(2)}) async-start(bf16[8,256,384]{2,1,0:T(8,128)(2,1)} %bitcast.32), calls=%async_computation.2 | async-start | bytes 3145728 | tf_op jit(solution)/shard_map/all_to_all | solution.py:473
  127.2 17.5 %collective-permute-start.16 = (bf16[512,256]{1,0:T(8,128)(2,1)S(1)}, bf16[512,256]{1,0:T(8,128)(2,1)S(1)}, u32[]{:S(2)}, u32[]{:S(2)}) collective-permute-start(bf16[512,256]{1,0:T(8,128)(2,1)S(1)} %get-tuple-element.90), channel_id=1, source_target_pairs={{0,8},{8,0},{16,24},{24,16},{1,9},{9,1},{17,25},{25,17},{2,10},{10... | collective-permute-start | bytes 786440 | tf_op jit(solution)/shard_map/ppermute | solution.py:639
  127.2 17.5 %collective-permute-start.17 = (bf16[512,256]{1,0:T(8,128)(2,1)S(1)}, bf16[512,256]{1,0:T(8,128)(2,1)S(1)}, u32[]{:S(2)}, u32[]{:S(2)}) collective-permute-start(bf16[512,256]{1,0:T(8,128)(2,1)S(1)} %get-tuple-element.91), channel_id=1, source_target_pairs={{0,16},{8,24},{16,0},{24,8},{1,17},{9,25},{17,1},{25,9},{2,18},{10... | collective-permute-start | bytes 786440 | tf_op jit(solution)/shard_map/ppermute | solution.py:639
  127.6 26.4 %collective-permute-start.18 = (bf16[512,256]{1,0:T(8,128)(2,1)S(1)}, bf16[512,256]{1,0:T(8,128)(2,1)S(1)}, u32[]{:S(2)}, u32[]{:S(2)}) collective-permute-start(bf16[512,256]{1,0:T(8,128)(2,1)S(1)} %get-tuple-element.92), channel_id=1, source_target_pairs={{0,24},{8,16},{16,8},{24,0},{1,25},{9,17},{17,9},{25,1},{2,26},{10... | collective-permute-start | bytes 786440 | tf_op jit(solution)/shard_map/ppermute | solution.py:639
  154.2 11.5 %collective-permute-start.21 = (bf16[512,256]{1,0:T(8,128)(2,1)S(1)}, bf16[512,256]{1,0:T(8,128)(2,1)S(1)}, u32[]{:S(2)}, u32[]{:S(2)}) collective-permute-start(bf16[512,256]{1,0:T(8,128)(2,1)S(1)} %add_convert_fusion.refs_0_), channel_id=1, source_target_pairs={{0,6},{1,7},{2,4},{3,5},{4,2},{5,3},{6,0},{7,1},{8,14},{9,15},{10,... | collective-permute-start | bytes 786440 | tf_op jit(solution)/shard_map/ppermute | solution.py:494
  156.8 11.6 %collective-permute-start.20 = (bf16[512,256]{1,0:T(8,128)(2,1)S(1)}, bf16[512,256]{1,0:T(8,128)(2,1)S(1)}, u32[]{:S(2)}, u32[]{:S(2)}) collective-permute-start(bf16[512,256]{1,0:T(8,128)(2,1)S(1)} %add_convert_fusion.refs_0_), channel_id=1, source_target_pairs={{0,4},{1,5},{2,6},{3,7},{4,0},{5,1},{6,2},{7,3},{8,12},{9,13},{10,... | collective-permute-start | bytes 786440 | tf_op jit(solution)/shard_map/ppermute | solution.py:494
  157.4 11.7 %collective-permute-start.19 = (bf16[512,256]{1,0:T(8,128)(2,1)S(1)}, bf16[512,256]{1,0:T(8,128)(2,1)S(1)}, u32[]{:S(2)}, u32[]{:S(2)}) collective-permute-start(bf16[512,256]{1,0:T(8,128)(2,1)S(1)} %add_convert_fusion.refs_0_), channel_id=1, source_target_pairs={{0,2},{1,3},{2,0},{3,1},{4,6},{5,7},{6,4},{7,5},{8,10},{9,11},{10,... | collective-permute-start | bytes 786440 | tf_op jit(solution)/shard_map/ppermute | solution.py:494
  169.8 24.5 %all-to-all-start.3 = ((bf16[8,256,384]{2,1,0:T(8,128)(2,1)}), bf16[8,256,384]{2,1,0:T(8,128)(2,1)S(1)}, u32[]{:S(2)}, u32[]{:S(2)}) async-start(bf16[8,256,384]{2,1,0:T(8,128)(2,1)} %bitcast.33), calls=%async_computation.3 | async-start | bytes 3145728 | tf_op jit(solution)/shard_map/all_to_all | solution.py:473
  (22 other events, 250.9 us)

commit v2 on v1

--- a/solution.py
+++ b/solution.py
@@ -370,7 +370,7 @@
     )(adjacency, counts, packed, grad, attn_out, stats, *carried)
 
 
-STEPS = 4
+STEPS = 2
 
 
 def pack_kernel(queries, keys, values, out_grad, weight, packed, top, bottom, own):
@@ -432,12 +432,12 @@
 
 def unpack(first, second):
     groups, tokens, _ = first.shape
-    height = tokens // 4
+    height = tokens // STEPS
     taken = pl.BlockSpec((groups, height, 3 * PAIR), lambda step: (0, step, 0))
     given = pl.BlockSpec((height, groups * 2 * PAIR), lambda step: (step, 0))
     return pl.pallas_call(
         unpack_kernel,
-        grid=(4,),
+        grid=(STEPS,),
         in_specs=[taken] * 2,
         out_specs=[given] * 3,
         out_shape=[jax.ShapeDtypeStruct((tokens, groups * 2 * PAIR), first.dtype)] * 3,

time: 198 us -> 196 us (0.990)
  Pallas kernels: 80 us -> 76.5 us
  transfers between devices with their start and end apart: 30 -> 30, of which waited for: 13 -> 13; matrix products, arithmetic and copies ran while one was open for 1% -> 1% of each run, Pallas kernels for 33% -> 32%
where the time goes in v2:
time: 196 us; the launch traced here: 195 us
  waiting for transfers between devices  78.8 us (40%)
  Pallas kernels  76.5 us (39%)
  starting transfers between devices  34.2 us (17%)
  local copies, waits for them, and re-layouts  3.17 us (2%)
    all_to_all x4, waiting for transfers between devices, exchange(): lax.all_to_all(chunks, 'seq', split_axis=0, concat_axis=0, tiled=True)  48.7 us
    pallas_call x3, Pallas kernels, backward(): pl.pallas_call(functools.partial(backward_kernel, blocks=blocks, begin=be...  38.5 us
    ppermute x20, waiting for transfers between devices, swap(): return lax.ppermute(array, 'seq', routes)  20.3 us
    pallas_call x2, Pallas kernels, forward(): pl.pallas_call(functools.partial(forward_kernel, begin=begin, end=end), i...  20.2 us
    all_to_all x4, starting transfers between devices, exchange(): lax.all_to_all(chunks, 'seq', split_axis=0, concat_axis=0, tiled=True)  15.1 us
    ppermute x20, starting transfers between devices, swap(): return lax.ppermute(array, 'seq', routes)  10.7 us
    ppermute x3, waiting for transfers between devices, pair_device(): lax.ppermute(parts[offset], 'fsdp', [(z, z ^ offset) for z in range(plane...  9.85 us
    pallas_call x1, Pallas kernels, project(): pl.pallas_call(functools.partial(project_kernel, places), in_specs=[far]...  7.29 us
  transfers between devices with their start and end apart: 30, of which 13 were waited for; matrix products, arithmetic and copies ran while one was open for 1% of the time, Pallas kernels for 32%

profile of v2, /device:TPU:16, one launch (start us, length us, event | category | flops | bytes accessed | tf_op | source)
XLA Modules:
  0.0 195.0 jit_solution(6511677210168042035)
XLA Ops:
  0.6 4.5 %pack.1 = (bf16[8,256,768]{2,1,0:T(8,128)(2,1)}, bf16[128,2048]{1,0:T(8,128)(2,1)}, bf16[128,2048]{1,0:T(8,128)(2,1)}, bf16[256,2048]{1,0:T(8,128)(2,1)}) custom-call(bf16[256,2048]{1,0:T(8,128)(2,1)} %bitcast.34, bf16[256,2048]{1,0:T(8,128)(2,1)} %bitcast.35, bf16[256,2048]{1,0:T(8,128)(2,1)} %bitcast.36, bf16[256,2048]{1,0:T(8,128)(2,1)} %bitcast.19, ...), custom_call_target="tpu_custom_call" | custom-call | tf_op jit(solution)/shard_map/pack/pallas_call | solution.py:404
  5.2 3.9 %all-to-all-start = ((bf16[8,256,768]{2,1,0:T(8,128)(2,1)}), bf16[8,256,768]{2,1,0:T(8,128)(2,1)S(1)}, u32[]{:S(2)}, u32[]{:S(2)}) async-start(bf16[8,256,768]{2,1,0:T(8,128)(2,1)} %get-tuple-element.56), calls=%async_computation | async-start | bytes 6291456 | tf_op jit(solution)/shard_map/all_to_all | solution.py:473
  9.5 1.6 collective-permute-start
  12.6 34.3 %all-to-all-done = bf16[8,256,768]{2,1,0:T(8,128)(2,1)S(1)} async-done(((bf16[8,256,768]{2,1,0:T(8,128)(2,1)}), bf16[8,256,768]{2,1,0:T(8,128)(2,1)S(1)}, u32[]{:S(2)}, u32[]{:S(2)}) %all-to-all-start) | async-done | bytes 3145760 | tf_op jit(solution)/shard_map/all_to_all | solution.py:473
  49.4 1.5 collective-permute-start.4
  51.0 10.1 %attend_forward.2 = (bf16[2048,128]{1,0:T(8,128)(2,1)S(1)}, bf16[2048,128]{1,0:T(8,128)(2,1)S(1)}, f32[2,128,256]{2,1,0:T(8,128)S(1)}) custom-call(s32[16,10]{1,0:T(8,128)S(1)} %bitcast.22, s32[16]{0:T(128)S(1)} %bitcast.30, bf16[2048,768]{1,0:T(8,128)(2,1)S(1)} %bitcast.14), custom_call_target="tpu_custom_call" | custom-call | flops 5368709120 | bytes 1572864 | tf_op jit(solution)/shard_map/attend_forward/pallas_call | solution.py:315
  62.5 1.8 collective-permute-start.15
  64.4 10.1 %attend_forward.3 = (bf16[2048,128]{1,0:T(8,128)(2,1)S(1)}, bf16[2048,128]{1,0:T(8,128)(2,1)S(1)}, f32[2,128,256]{2,1,0:T(8,128)S(1)}) custom-call(s32[16,10]{1,0:T(8,128)S(1)} %bitcast.23, s32[16]{0:T(128)S(1)} %bitcast.31, bf16[2048,768]{1,0:T(8,128)(2,1)S(1)} %bitcast.15, bf16[2048,128]{1,0:T(8,128)(2,1)S(1)} %get-tuple-element.66.refs_0_, ...), custom_call_target="tpu_custom_call" | custom-call | flops 5368709120 | bytes 1572864 | tf_op jit(solution)/shard_map/attend_forward/pallas_call | solution.py:315
  78.0 11.6 %collective-permute-done.11.refs_10_ = bf16[128,2048]{1,0:T(8,128)(2,1)S(1)} collective-permute-done((bf16[128,2048]{1,0:T(8,128)(2,1)S(1)}, bf16[128,2048]{1,0:T(8,128)(2,1)S(1)}, u32[]{:S(2)}, u32[]{:S(2)}) %collective-permute-start.11) | collective-permute-done | bytes 524320 | tf_op jit(solution)/shard_map/ppermute | solution.py:494
  90.2 1.4 collective-permute-done.12.refs_11_
  92.3 7.3 %project.1 = (bf16[2048,256]{1,0:T(8,128)(2,1)S(1)}, bf16[8,256,256]{2,1,0:T(8,128)(2,1)}) custom-call(bf16[256,2048]{1,0:T(8,128)(2,1)S(1)} %bitcast.21, bf16[256,2048]{1,0:T(8,128)(2,1)} %collective-permute-done.1.refs_1_, bf16[128,2048]{1,0:T(8,128)(2,1)S(1)} %collective-permute-done.3.refs_2_, bf16[128,2048]{1,0:T(8,128)(2,1)S(1)} %collective-permute-done.7.refs_3_, ...), custom_call_target="tpu_custom_call" | custom-call | flops 4294967296 | bytes 12582912 | tf_op jit(solution)/shard_map/project/pallas_call | solution.py:549
  100.6 3.6 %all-to-all-start.1 = ((bf16[8,256,256]{2,1,0:T(8,128)(2,1)}), bf16[8,256,256]{2,1,0:T(8,128)(2,1)S(1)}, u32[]{:S(2)}, u32[]{:S(2)}) async-start(bf16[8,256,256]{2,1,0:T(8,128)(2,1)} %get-tuple-element.84), calls=%async_computation.1 | async-start | bytes 2097152 | tf_op jit(solution)/shard_map/all_to_all | solution.py:473
  104.2 17.0 %attend_backward.3 = bf16[2048,384]{1,0:T(8,128)(2,1)} custom-call(s32[16,10]{1,0:T(8,128)} %bitcast.24, s32[16]{0:T(128)} %bitcast.27, bf16[2048,768]{1,0:T(8,128)(2,1)} %bitcast.16, bf16[2048,256]{1,0:T(8,128)(2,1)} %copy-done.5, bf16[2048,128]{1,0:T(8,128)(2,1)} %copy-done.7, f32[2,128,256]{2,1,0:T(8,128)} %copy-done.8), custom_call_target="tpu_custom_call" | custom-call | flops 13421772800 | bytes 3145728 | tf_op jit(solution)/shard_map/attend_backward/pallas_call | solution.py:349
  121.2 4.1 %all-to-all-start.2 = ((bf16[8,256,384]{2,1,0:T(8,128)(2,1)}), bf16[8,256,384]{2,1,0:T(8,128)(2,1)S(1)}, u32[]{:S(2)}, u32[]{:S(2)}) async-start(bf16[8,256,384]{2,1,0:T(8,128)(2,1)} %bitcast.32), calls=%async_computation.2 | async-start | bytes 3145728 | tf_op jit(solution)/shard_map/all_to_all | solution.py:473
  126.6 2.3 %collective-permute-start.18 = (bf16[512,256]{1,0:T(8,128)(2,1)S(1)}, bf16[512,256]{1,0:T(8,128)(2,1)S(1)}, u32[]{:S(2)}, u32[]{:S(2)}) collective-permute-start(bf16[512,256]{1,0:T(8,128)(2,1)S(1)} %get-tuple-element.92), channel_id=1, source_target_pairs={{0,24},{8,16},{16,8},{24,0},{1,25},{9,17},{17,9},{25,1},{2,26},{10... | collective-permute-start | bytes 786440 | tf_op jit(solution)/shard_map/ppermute | solution.py:639
  128.9 13.5 %attend_backward.4 = (bf16[2048,128]{1,0:T(8,128)(2,1)}, f32[2048,128]{1,0:T(8,128)}, f32[2048,128]{1,0:T(8,128)}) custom-call(s32[16,10]{1,0:T(8,128)} %bitcast.25, s32[16]{0:T(128)} %bitcast.28, bf16[2048,768]{1,0:T(8,128)(2,1)} %bitcast.17, bf16[2048,256]{1,0:T(8,128)(2,1)} %copy-done.5, bf16[2048,128]{1,0:T(8,128)(2,1)} %copy-done.6, ...), custom_call_target="tpu_custom_call" | custom-call | flops 10066329600 | bytes 2359296 | tf_op jit(solution)/shard_map/attend_backward/pallas_call | solution.py:349
  142.4 9.8 %collective-permute-done.18 = bf16[512,256]{1,0:T(8,128)(2,1)S(1)} collective-permute-done((bf16[512,256]{1,0:T(8,128)(2,1)S(1)}, bf16[512,256]{1,0:T(8,128)(2,1)S(1)}, u32[]{:S(2)}, u32[]{:S(2)}) %collective-permute-start.18) | collective-permute-done | bytes 262176 | tf_op jit(solution)/shard_map/ppermute | solution.py:639
  152.4 2.6 %collective-permute-start.21 = (bf16[512,256]{1,0:T(8,128)(2,1)S(1)}, bf16[512,256]{1,0:T(8,128)(2,1)S(1)}, u32[]{:S(2)}, u32[]{:S(2)}) collective-permute-start(bf16[512,256]{1,0:T(8,128)(2,1)S(1)} %add_convert_fusion.refs_0_), channel_id=1, source_target_pairs={{0,6},{1,7},{2,4},{3,5},{4,2},{5,3},{6,0},{7,1},{8,14},{9,15},{10,... | collective-permute-start | bytes 786440 | tf_op jit(solution)/shard_map/ppermute | solution.py:494
  155.9 8.1 %attend_backward.5 = bf16[2048,384]{1,0:T(8,128)(2,1)} custom-call(s32[16,10]{1,0:T(8,128)} %bitcast.26, s32[16]{0:T(128)} %bitcast.29, bf16[2048,768]{1,0:T(8,128)(2,1)} %bitcast.18, bf16[2048,256]{1,0:T(8,128)(2,1)} %copy-done.5, bf16[2048,128]{1,0:T(8,128)(2,1)} %copy-done.6, f32[2,128,256]{2,1,0:T(8,128)} %copy-done.8, ...), custom_call_target="tpu_custom_call" | custom-call | flops 3355443200 | bytes 786432 | tf_op jit(solution)/shard_map/attend_backward/pallas_call | solution.py:349
  164.0 2.6 %collective-permute-done.20.refs_4_ = bf16[512,256]{1,0:T(8,128)(2,1)S(1)} collective-permute-done((bf16[512,256]{1,0:T(8,128)(2,1)S(1)}, bf16[512,256]{1,0:T(8,128)(2,1)S(1)}, u32[]{:S(2)}, u32[]{:S(2)}) %collective-permute-start.20) | collective-permute-done | bytes 262176 | tf_op jit(solution)/shard_map/ppermute | solution.py:494
  168.0 3.6 %all-to-all-start.3 = ((bf16[8,256,384]{2,1,0:T(8,128)(2,1)}), bf16[8,256,384]{2,1,0:T(8,128)(2,1)S(1)}, u32[]{:S(2)}, u32[]{:S(2)}) async-start(bf16[8,256,384]{2,1,0:T(8,128)(2,1)} %bitcast.33), calls=%async_computation.3 | async-start | bytes 3145728 | tf_op jit(solution)/shard_map/all_to_all | solution.py:473
  174.7 3.4 %spread.1 = f32[512,2048]{1,0:T(8,128)} custom-call(bf16[512,256]{1,0:T(8,128)(2,1)} %copy-done.9, bf16[512,256]{1,0:T(8,128)(2,1)} %copy-done.13, bf16[512,256]{1,0:T(8,128)(2,1)} %copy-done.12, bf16[512,256]{1,0:T(8,128)(2,1)} %copy-done.14, bf16[512,256]{1,0:T(8,128)(2,1)} %copy-done.11, bf16[512,256]{1,0:T(8,128)(2,1)} %collective-permute-done.24.refs_5_, ...), custom_call_target="tpu_custom_call" | custom-call | tf_op jit(solution)/shard_map/spread/pallas_call | solution.py:461
  178.2 14.3 %all-to-all-done.3.second = bf16[8,256,384]{2,1,0:T(8,128)(2,1)S(1)} async-done(((bf16[8,256,384]{2,1,0:T(8,128)(2,1)}), bf16[8,256,384]{2,1,0:T(8,128)(2,1)S(1)}, u32[]{:S(2)}, u32[]{:S(2)}) %all-to-all-start.3) | async-done | bytes 1572896 | tf_op jit(solution)/shard_map/all_to_all | solution.py:473
  192.5 2.4 %unpack.1 = (bf16[256,2048]{1,0:T(8,128)(2,1)}, bf16[256,2048]{1,0:T(8,128)(2,1)}, bf16[256,2048]{1,0:T(8,128)(2,1)}) custom-call(bf16[8,256,384]{2,1,0:T(8,128)(2,1)S(1)} %all-to-all-done.2.first, bf16[8,256,384]{2,1,0:T(8,128)(2,1)S(1)} %all-to-all-done.3.second), custom_call_target="tpu_custom_call" | custom-call | tf_op jit(solution)/shard_map/unpack/pallas_call | solution.py:438
  (81 shorter events, 18.5 us)
Async XLA Ops:
  5.2 41.8 %all-to-all-start = ((bf16[8,256,768]{2,1,0:T(8,128)(2,1)}), bf16[8,256,768]{2,1,0:T(8,128)(2,1)S(1)}, u32[]{:S(2)}, u32[]{:S(2)}) async-start(bf16[8,256,768]{2,1,0:T(8,128)(2,1)} %get-tuple-element.56), calls=%async_computation | async-start | bytes 6291456 | tf_op jit(solution)/shard_map/all_to_all | solution.py:473
  9.0 3.6 %collective-permute-start.1 = (bf16[256,2048]{1,0:T(8,128)(2,1)}, bf16[256,2048]{1,0:T(8,128)(2,1)}, u32[]{:S(2)}, u32[]{:S(2)}) collective-permute-start(bf16[256,2048]{1,0:T(8,128)(2,1)} %bitcast.20), channel_id=1, source_target_pairs={{0,1},{1,0},{2,3},{3,2},{4,5},{5,4},{6,7},{7,6},{8,9},{9,8},{10,11... | collective-permute-start | bytes 3145736 | tf_op jit(solution)/shard_map/ppermute | solution.py:494
  9.5 3.1 %collective-permute-start = (bf16[256,2048]{1,0:T(8,128)(2,1)}, bf16[256,2048]{1,0:T(8,128)(2,1)}, u32[]{:S(2)}, u32[]{:S(2)}) collective-permute-start(bf16[256,2048]{1,0:T(8,128)(2,1)} %get-tuple-element.59.refs_14_), channel_id=1, source_target_pairs={{0,8},{1,9},{10,18},{11,19},{20,12},{21,13},{30,22},{31,23}} | collective-permute-start | bytes 3145736 | tf_op jit(solution)/shard_map/ppermute | solution.py:489
  11.2 49.9 %collective-permute-start.2 = (bf16[256,2048]{1,0:T(8,128)(2,1)}, bf16[256,2048]{1,0:T(8,128)(2,1)}, u32[]{:S(2)}, u32[]{:S(2)}) collective-permute-start(bf16[256,2048]{1,0:T(8,128)(2,1)} %get-tuple-element.59.refs_14_), channel_id=1, source_target_pairs={{0,16},{1,17},{10,26},{11,27},{20,4},{21,5},{30,14},{31,15}} | collective-permute-start | bytes 3145736 | tf_op jit(solution)/shard_map/ppermute | solution.py:489
  46.9 28.2 %collective-permute-start.5 = (bf16[128,2048]{1,0:T(8,128)(2,1)}, bf16[128,2048]{1,0:T(8,128)(2,1)S(1)}, u32[]{:S(2)}, u32[]{:S(2)}) collective-permute-start(bf16[128,2048]{1,0:T(8,128)(2,1)} %get-tuple-element.72), channel_id=1, source_target_pairs={{0,4},{1,5},{2,6},{3,7},{4,0},{5,1},{6,2},{7,3},{8,12},{9,13},{10,... | collective-permute-start | bytes 1572872 | tf_op jit(solution)/shard_map/ppermute | solution.py:494
  47.5 27.7 %collective-permute-start.3 = (bf16[128,2048]{1,0:T(8,128)(2,1)}, bf16[128,2048]{1,0:T(8,128)(2,1)S(1)}, u32[]{:S(2)}, u32[]{:S(2)}) collective-permute-start(bf16[128,2048]{1,0:T(8,128)(2,1)} %get-tuple-element.72), channel_id=1, source_target_pairs={{0,2},{1,3},{2,0},{3,1},{4,6},{5,7},{6,4},{7,5},{8,10},{9,11},{10,... | collective-permute-start | bytes 1572872 | tf_op jit(solution)/shard_map/ppermute | solution.py:494
  48.1 27.1 %collective-permute-start.6 = (bf16[128,2048]{1,0:T(8,128)(2,1)}, bf16[128,2048]{1,0:T(8,128)(2,1)S(1)}, u32[]{:S(2)}, u32[]{:S(2)}) collective-permute-start(bf16[128,2048]{1,0:T(8,128)(2,1)} %get-tuple-element.73), channel_id=1, source_target_pairs={{0,4},{1,5},{2,6},{3,7},{4,0},{5,1},{6,2},{7,3},{8,12},{9,13},{10,... | collective-permute-start | bytes 1572872 | tf_op jit(solution)/shard_map/ppermute | solution.py:494
  49.4 25.7 %collective-permute-start.4 = (bf16[128,2048]{1,0:T(8,128)(2,1)}, bf16[128,2048]{1,0:T(8,128)(2,1)S(1)}, u32[]{:S(2)}, u32[]{:S(2)}) collective-permute-start(bf16[128,2048]{1,0:T(8,128)(2,1)} %get-tuple-element.73), channel_id=1, source_target_pairs={{0,2},{1,3},{2,0},{3,1},{4,6},{5,7},{6,4},{7,5},{8,10},{9,11},{10,... | collective-permute-start | bytes 1572872 | tf_op jit(solution)/shard_map/ppermute | solution.py:494
  62.5 27.7 %collective-permute-start.15 = (bf16[256,2048]{1,0:T(8,128)(2,1)S(1)}, bf16[256,2048]{1,0:T(8,128)(2,1)S(1)}, u32[]{:S(2)}, u32[]{:S(2)}) collective-permute-start(bf16[256,2048]{1,0:T(8,128)(2,1)S(1)} %broadcast_select_fusion), channel_id=1, source_target_pairs={{16,24},{17,25},{10,2},{11,3},{20,28},{21,29},{14,6},{15,7}} | collective-permute-start | bytes 3145736 | tf_op jit(solution)/shard_map/ppermute | solution.py:489
  75.2 2.6 %collective-permute-start.9 = (bf16[128,2048]{1,0:T(8,128)(2,1)S(1)}, bf16[128,2048]{1,0:T(8,128)(2,1)S(1)}, u32[]{:S(2)}, u32[]{:S(2)}) collective-permute-start(bf16[128,2048]{1,0:T(8,128)(2,1)S(1)} %collective-permute-done.5.refs_6_), channel_id=1, source_target_pairs={{0,1},{1,0},{2,3},{3,2},{4,5},{5,4},{6,7},{7,6},{8,9},{9,8},{10,11... | collective-permute-start | bytes 1572872 | tf_op jit(solution)/shard_map/ppermute | solution.py:494
  75.7 13.9 %collective-permute-start.11 = (bf16[128,2048]{1,0:T(8,128)(2,1)S(1)}, bf16[128,2048]{1,0:T(8,128)(2,1)S(1)}, u32[]{:S(2)}, u32[]{:S(2)}) collective-permute-start(bf16[128,2048]{1,0:T(8,128)(2,1)S(1)} %collective-permute-done.3.refs_2_), channel_id=1, source_target_pairs={{0,4},{1,5},{2,6},{3,7},{4,0},{5,1},{6,2},{7,3},{8,12},{9,13},{10,... | collective-permute-start | bytes 1572872 | tf_op jit(solution)/shard_map/ppermute | solution.py:494
  75.7 13.9 %collective-permute-start.13 = (bf16[128,2048]{1,0:T(8,128)(2,1)S(1)}, bf16[128,2048]{1,0:T(8,128)(2,1)S(1)}, u32[]{:S(2)}, u32[]{:S(2)}) collective-permute-start(bf16[128,2048]{1,0:T(8,128)(2,1)S(1)} %collective-permute-done.6.refs_8_), channel_id=1, source_target_pairs={{0,2},{1,3},{2,0},{3,1},{4,6},{5,7},{6,4},{7,5},{8,10},{9,11},{10,... | collective-permute-start | bytes 1572872 | tf_op jit(solution)/shard_map/ppermute | solution.py:494
  77.1 13.0 %collective-permute-start.7 = (bf16[128,2048]{1,0:T(8,128)(2,1)S(1)}, bf16[128,2048]{1,0:T(8,128)(2,1)S(1)}, u32[]{:S(2)}, u32[]{:S(2)}) collective-permute-start(bf16[128,2048]{1,0:T(8,128)(2,1)S(1)} %collective-permute-done.3.refs_2_), channel_id=1, source_target_pairs={{0,1},{1,0},{2,3},{3,2},{4,5},{5,4},{6,7},{7,6},{8,9},{9,8},{10,11... | collective-permute-start | bytes 1572872 | tf_op jit(solution)/shard_map/ppermute | solution.py:494
  77.9 12.3 %collective-permute-start.10 = (bf16[128,2048]{1,0:T(8,128)(2,1)S(1)}, bf16[128,2048]{1,0:T(8,128)(2,1)S(1)}, u32[]{:S(2)}, u32[]{:S(2)}) collective-permute-start(bf16[128,2048]{1,0:T(8,128)(2,1)S(1)} %collective-permute-done.6.refs_8_), channel_id=1, source_target_pairs={{0,1},{1,0},{2,3},{3,2},{4,5},{5,4},{6,7},{7,6},{8,9},{9,8},{10,11... | collective-permute-start | bytes 1572872 | tf_op jit(solution)/shard_map/ppermute | solution.py:494
  89.7 2.7 %collective-permute-start.14 = (bf16[128,2048]{1,0:T(8,128)(2,1)S(1)}, bf16[128,2048]{1,0:T(8,128)(2,1)S(1)}, u32[]{:S(2)}, u32[]{:S(2)}) collective-permute-start(bf16[128,2048]{1,0:T(8,128)(2,1)S(1)} %collective-permute-done.13.refs_12_), channel_id=1, source_target_pairs={{0,1},{1,0},{2,3},{3,2},{4,5},{5,4},{6,7},{7,6},{8,9},{9,8},{10,11... | collective-permute-start | bytes 1572872 | tf_op jit(solution)/shard_map/ppermute | solution.py:494
  100.6 20.6 %all-to-all-start.1 = ((bf16[8,256,256]{2,1,0:T(8,128)(2,1)}), bf16[8,256,256]{2,1,0:T(8,128)(2,1)S(1)}, u32[]{:S(2)}, u32[]{:S(2)}) async-start(bf16[8,256,256]{2,1,0:T(8,128)(2,1)} %get-tuple-element.84), calls=%async_computation.1 | async-start | bytes 2097152 | tf_op jit(solution)/shard_map/all_to_all | solution.py:473
  121.2 46.1 %all-to-all-start.2 = ((bf16[8,256,384]{2,1,0:T(8,128)(2,1)}), bf16[8,256,384]{2,1,0:T(8,128)(2,1)S(1)}, u32[]{:S(2)}, u32[]{:S(2)}) async-start(bf16[8,256,384]{2,1,0:T(8,128)(2,1)} %bitcast.32), calls=%async_computation.2 | async-start | bytes 3145728 | tf_op jit(solution)/shard_map/all_to_all | solution.py:473
  125.4 17.0 %collective-permute-start.16 = (bf16[512,256]{1,0:T(8,128)(2,1)S(1)}, bf16[512,256]{1,0:T(8,128)(2,1)S(1)}, u32[]{:S(2)}, u32[]{:S(2)}) collective-permute-start(bf16[512,256]{1,0:T(8,128)(2,1)S(1)} %get-tuple-element.90), channel_id=1, source_target_pairs={{0,8},{8,0},{16,24},{24,16},{1,9},{9,1},{17,25},{25,17},{2,10},{10... | collective-permute-start | bytes 786440 | tf_op jit(solution)/shard_map/ppermute | solution.py:639
  125.4 16.9 %collective-permute-start.17 = (bf16[512,256]{1,0:T(8,128)(2,1)S(1)}, bf16[512,256]{1,0:T(8,128)(2,1)S(1)}, u32[]{:S(2)}, u32[]{:S(2)}) collective-permute-start(bf16[512,256]{1,0:T(8,128)(2,1)S(1)} %get-tuple-element.91), channel_id=1, source_target_pairs={{0,16},{8,24},{16,0},{24,8},{1,17},{9,25},{17,1},{25,9},{2,18},{10... | collective-permute-start | bytes 786440 | tf_op jit(solution)/shard_map/ppermute | solution.py:639
  126.6 25.6 %collective-permute-start.18 = (bf16[512,256]{1,0:T(8,128)(2,1)S(1)}, bf16[512,256]{1,0:T(8,128)(2,1)S(1)}, u32[]{:S(2)}, u32[]{:S(2)}) collective-permute-start(bf16[512,256]{1,0:T(8,128)(2,1)S(1)} %get-tuple-element.92), channel_id=1, source_target_pairs={{0,24},{8,16},{16,8},{24,0},{1,25},{9,17},{17,9},{25,1},{2,26},{10... | collective-permute-start | bytes 786440 | tf_op jit(solution)/shard_map/ppermute | solution.py:639
  152.4 11.6 %collective-permute-start.21 = (bf16[512,256]{1,0:T(8,128)(2,1)S(1)}, bf16[512,256]{1,0:T(8,128)(2,1)S(1)}, u32[]{:S(2)}, u32[]{:S(2)}) collective-permute-start(bf16[512,256]{1,0:T(8,128)(2,1)S(1)} %add_convert_fusion.refs_0_), channel_id=1, source_target_pairs={{0,6},{1,7},{2,4},{3,5},{4,2},{5,3},{6,0},{7,1},{8,14},{9,15},{10,... | collective-permute-start | bytes 786440 | tf_op jit(solution)/shard_map/ppermute | solution.py:494
  155.0 11.6 %collective-permute-start.20 = (bf16[512,256]{1,0:T(8,128)(2,1)S(1)}, bf16[512,256]{1,0:T(8,128)(2,1)S(1)}, u32[]{:S(2)}, u32[]{:S(2)}) collective-permute-start(bf16[512,256]{1,0:T(8,128)(2,1)S(1)} %add_convert_fusion.refs_0_), channel_id=1, source_target_pairs={{0,4},{1,5},{2,6},{3,7},{4,0},{5,1},{6,2},{7,3},{8,12},{9,13},{10,... | collective-permute-start | bytes 786440 | tf_op jit(solution)/shard_map/ppermute | solution.py:494
  155.6 11.7 %collective-permute-start.19 = (bf16[512,256]{1,0:T(8,128)(2,1)S(1)}, bf16[512,256]{1,0:T(8,128)(2,1)S(1)}, u32[]{:S(2)}, u32[]{:S(2)}) collective-permute-start(bf16[512,256]{1,0:T(8,128)(2,1)S(1)} %add_convert_fusion.refs_0_), channel_id=1, source_target_pairs={{0,2},{1,3},{2,0},{3,1},{4,6},{5,7},{6,4},{7,5},{8,10},{9,11},{10,... | collective-permute-start | bytes 786440 | tf_op jit(solution)/shard_map/ppermute | solution.py:494
  168.0 24.5 %all-to-all-start.3 = ((bf16[8,256,384]{2,1,0:T(8,128)(2,1)}), bf16[8,256,384]{2,1,0:T(8,128)(2,1)S(1)}, u32[]{:S(2)}, u32[]{:S(2)}) async-start(bf16[8,256,384]{2,1,0:T(8,128)(2,1)} %bitcast.33), calls=%async_computation.3 | async-start | bytes 3145728 | tf_op jit(solution)/shard_map/all_to_all | solution.py:473
  (22 other events, 250.4 us)

commit v3 on v2

--- a/solution.py
+++ b/solution.py
@@ -298,6 +298,7 @@
 SMALL = pltpu.CompilerParams(vmem_limit_bytes=16 * 2**20)
 PARAMS = pltpu.CompilerParams(vmem_limit_bytes=32 * 2**20)
 WIDE = pltpu.CompilerParams(vmem_limit_bytes=60 * 2**20)
+BACKWARD = pltpu.CompilerParams(vmem_limit_bytes=60716 * 2**10)
 
 
 def cost(tokens, products):
@@ -364,7 +365,7 @@
             pltpu.VMEM(((end - begin) * 8, 2 * BLK), jnp.float32),
             pltpu.VMEM((end - begin, PAIR, 2 * BLK), jnp.float32),
         ],
-        compiler_params=WIDE,
+        compiler_params=BACKWARD,
         cost_estimate=cost(tokens * (end - begin) // blocks, 5),
         name="attend_backward",
     )(adjacency, counts, packed, grad, attn_out, stats, *carried)

time: 196 us -> 196 us (level)
  transfers between devices with their start and end apart: 30 -> 30, of which waited for: 13 -> 14; matrix products, arithmetic and copies ran while one was open for 1% -> 1% of each run, Pallas kernels for 32% -> 31%
where the time goes in v3:
time: 196 us; the launch traced here: 194 us
  waiting for transfers between devices  79.2 us (40%)
  Pallas kernels  75.3 us (38%)
  starting transfers between devices  34.6 us (18%)
  local copies, waits for them, and re-layouts  2.49 us (1%)
    all_to_all x4, waiting for transfers between devices, exchange(): lax.all_to_all(chunks, 'seq', split_axis=0, concat_axis=0, tiled=True)  48.7 us
    pallas_call x3, Pallas kernels, backward(): pl.pallas_call(functools.partial(backward_kernel, blocks=blocks, begin=be...  38 us
    ppermute x20, waiting for transfers between devices, swap(): return lax.ppermute(array, 'seq', routes)  20.6 us
    pallas_call x2, Pallas kernels, forward(): pl.pallas_call(functools.partial(forward_kernel, begin=begin, end=end), i...  19.5 us
    all_to_all x4, starting transfers between devices, exchange(): lax.all_to_all(chunks, 'seq', split_axis=0, concat_axis=0, tiled=True)  15.1 us
    ppermute x20, starting transfers between devices, swap(): return lax.ppermute(array, 'seq', routes)  10.6 us
    ppermute x3, waiting for transfers between devices, pair_device(): lax.ppermute(parts[offset], 'fsdp', [(z, z ^ offset) for z in range(plane...  9.96 us
    pallas_call x1, Pallas kernels, project(): pl.pallas_call(functools.partial(project_kernel, places), in_specs=[far]...  7.29 us
  transfers between devices with their start and end apart: 30, of which 14 were waited for; matrix products, arithmetic and copies ran while one was open for 1% of the time, Pallas kernels for 31%

profile of v3, /device:TPU:16, one launch (start us, length us, event | category | flops | bytes accessed | tf_op | source)
XLA Modules:
  0.0 194.0 jit_solution(9123996014412915601)
XLA Ops:
  0.6 4.5 %pack.1 = (bf16[8,256,768]{2,1,0:T(8,128)(2,1)}, bf16[128,2048]{1,0:T(8,128)(2,1)}, bf16[128,2048]{1,0:T(8,128)(2,1)}, bf16[256,2048]{1,0:T(8,128)(2,1)}) custom-call(bf16[256,2048]{1,0:T(8,128)(2,1)} %bitcast.34, bf16[256,2048]{1,0:T(8,128)(2,1)} %bitcast.35, bf16[256,2048]{1,0:T(8,128)(2,1)} %bitcast.36, bf16[256,2048]{1,0:T(8,128)(2,1)} %bitcast.19, ...), custom_call_target="tpu_custom_call" | custom-call | tf_op jit(solution)/shard_map/pack/pallas_call | solution.py:405
  5.2 3.9 %all-to-all-start = ((bf16[8,256,768]{2,1,0:T(8,128)(2,1)}), bf16[8,256,768]{2,1,0:T(8,128)(2,1)S(1)}, u32[]{:S(2)}, u32[]{:S(2)}) async-start(bf16[8,256,768]{2,1,0:T(8,128)(2,1)} %get-tuple-element.56), calls=%async_computation | async-start | bytes 6291456 | tf_op jit(solution)/shard_map/all_to_all | solution.py:474
  9.5 1.6 collective-permute-start
  12.6 34.3 %all-to-all-done = bf16[8,256,768]{2,1,0:T(8,128)(2,1)S(1)} async-done(((bf16[8,256,768]{2,1,0:T(8,128)(2,1)}), bf16[8,256,768]{2,1,0:T(8,128)(2,1)S(1)}, u32[]{:S(2)}, u32[]{:S(2)}) %all-to-all-start) | async-done | bytes 3145760 | tf_op jit(solution)/shard_map/all_to_all | solution.py:474
  49.4 1.5 collective-permute-start.4
  51.0 10.6 %attend_forward.2 = (bf16[2048,128]{1,0:T(8,128)(2,1)S(1)}, bf16[2048,128]{1,0:T(8,128)(2,1)S(1)}, f32[2,128,256]{2,1,0:T(8,128)S(1)}) custom-call(s32[16,10]{1,0:T(8,128)S(1)} %bitcast.22, s32[16]{0:T(128)S(1)} %bitcast.30, bf16[2048,768]{1,0:T(8,128)(2,1)S(1)} %bitcast.14), custom_call_target="tpu_custom_call" | custom-call | flops 5368709120 | bytes 1572864 | tf_op jit(solution)/shard_map/attend_forward/pallas_call | solution.py:316
  63.0 2.4 %collective-permute-start.15 = (bf16[256,2048]{1,0:T(8,128)(2,1)S(1)}, bf16[256,2048]{1,0:T(8,128)(2,1)S(1)}, u32[]{:S(2)}, u32[]{:S(2)}) collective-permute-start(bf16[256,2048]{1,0:T(8,128)(2,1)S(1)} %broadcast_select_fusion), channel_id=1, source_target_pairs={{16,24},{17,25},{10,2},{11,3},{20,28},{21,29},{14,6},{15,7}} | collective-permute-start | bytes 3145736 | tf_op jit(solution)/shard_map/ppermute | solution.py:490
  65.5 8.9 %attend_forward.3 = (bf16[2048,128]{1,0:T(8,128)(2,1)S(1)}, bf16[2048,128]{1,0:T(8,128)(2,1)S(1)}, f32[2,128,256]{2,1,0:T(8,128)S(1)}) custom-call(s32[16,10]{1,0:T(8,128)S(1)} %bitcast.23, s32[16]{0:T(128)S(1)} %bitcast.31, bf16[2048,768]{1,0:T(8,128)(2,1)S(1)} %bitcast.15, bf16[2048,128]{1,0:T(8,128)(2,1)S(1)} %get-tuple-element.66.refs_0_, ...), custom_call_target="tpu_custom_call" | custom-call | flops 5368709120 | bytes 1572864 | tf_op jit(solution)/shard_map/attend_forward/pallas_call | solution.py:316
  78.0 11.6 %collective-permute-done.11.refs_10_ = bf16[128,2048]{1,0:T(8,128)(2,1)S(1)} collective-permute-done((bf16[128,2048]{1,0:T(8,128)(2,1)S(1)}, bf16[128,2048]{1,0:T(8,128)(2,1)S(1)}, u32[]{:S(2)}, u32[]{:S(2)}) %collective-permute-start.11) | collective-permute-done | bytes 524320 | tf_op jit(solution)/shard_map/ppermute | solution.py:495
  92.3 7.3 %project.1 = (bf16[2048,256]{1,0:T(8,128)(2,1)S(1)}, bf16[8,256,256]{2,1,0:T(8,128)(2,1)}) custom-call(bf16[256,2048]{1,0:T(8,128)(2,1)S(1)} %bitcast.21, bf16[256,2048]{1,0:T(8,128)(2,1)} %collective-permute-done.1.refs_1_, bf16[128,2048]{1,0:T(8,128)(2,1)S(1)} %collective-permute-done.3.refs_2_, bf16[128,2048]{1,0:T(8,128)(2,1)S(1)} %collective-permute-done.7.refs_3_, ...), custom_call_target="tpu_custom_call" | custom-call | flops 4294967296 | bytes 12582912 | tf_op jit(solution)/shard_map/project/pallas_call | solution.py:550
  100.6 3.6 %all-to-all-start.1 = ((bf16[8,256,256]{2,1,0:T(8,128)(2,1)}), bf16[8,256,256]{2,1,0:T(8,128)(2,1)S(1)}, u32[]{:S(2)}, u32[]{:S(2)}) async-start(bf16[8,256,256]{2,1,0:T(8,128)(2,1)} %get-tuple-element.84), calls=%async_computation.1 | async-start | bytes 2097152 | tf_op jit(solution)/shard_map/all_to_all | solution.py:474
  104.1 16.8 %attend_backward.3 = bf16[2048,384]{1,0:T(8,128)(2,1)} custom-call(s32[16,10]{1,0:T(8,128)} %bitcast.24, s32[16]{0:T(128)} %bitcast.27, bf16[2048,768]{1,0:T(8,128)(2,1)} %bitcast.16, bf16[2048,256]{1,0:T(8,128)(2,1)} %copy-done.5, bf16[2048,128]{1,0:T(8,128)(2,1)} %copy-done.7, f32[2,128,256]{2,1,0:T(8,128)} %copy-done.8), custom_call_target="tpu_custom_call" | custom-call | flops 13421772800 | bytes 3145728 | tf_op jit(solution)/shard_map/attend_backward/pallas_call | solution.py:350
  120.9 4.1 %all-to-all-start.2 = ((bf16[8,256,384]{2,1,0:T(8,128)(2,1)}), bf16[8,256,384]{2,1,0:T(8,128)(2,1)S(1)}, u32[]{:S(2)}, u32[]{:S(2)}) async-start(bf16[8,256,384]{2,1,0:T(8,128)(2,1)} %bitcast.32), calls=%async_computation.2 | async-start | bytes 3145728 | tf_op jit(solution)/shard_map/all_to_all | solution.py:474
  125.2 2.8 %collective-permute-start.17 = (bf16[512,256]{1,0:T(8,128)(2,1)S(1)}, bf16[512,256]{1,0:T(8,128)(2,1)S(1)}, u32[]{:S(2)}, u32[]{:S(2)}) collective-permute-start(bf16[512,256]{1,0:T(8,128)(2,1)S(1)} %get-tuple-element.91), channel_id=1, source_target_pairs={{0,16},{8,24},{16,0},{24,8},{1,17},{9,25},{17,1},{25,9},{2,18},{10... | collective-permute-start | bytes 786440 | tf_op jit(solution)/shard_map/ppermute | solution.py:640
  128.6 13.3 %attend_backward.4 = (bf16[2048,128]{1,0:T(8,128)(2,1)}, f32[2048,128]{1,0:T(8,128)}, f32[2048,128]{1,0:T(8,128)}) custom-call(s32[16,10]{1,0:T(8,128)} %bitcast.25, s32[16]{0:T(128)} %bitcast.28, bf16[2048,768]{1,0:T(8,128)(2,1)} %bitcast.17, bf16[2048,256]{1,0:T(8,128)(2,1)} %copy-done.5, bf16[2048,128]{1,0:T(8,128)(2,1)} %copy-done.6, ...), custom_call_target="tpu_custom_call" | custom-call | flops 10066329600 | bytes 2359296 | tf_op jit(solution)/shard_map/attend_backward/pallas_call | solution.py:350
  142.0 3.9 %collective-permute-done.17 = bf16[512,256]{1,0:T(8,128)(2,1)S(1)} collective-permute-done((bf16[512,256]{1,0:T(8,128)(2,1)S(1)}, bf16[512,256]{1,0:T(8,128)(2,1)S(1)}, u32[]{:S(2)}, u32[]{:S(2)}) %collective-permute-start.17) | collective-permute-done | bytes 262176 | tf_op jit(solution)/shard_map/ppermute | solution.py:640
  145.9 6.1 %collective-permute-done.18 = bf16[512,256]{1,0:T(8,128)(2,1)S(1)} collective-permute-done((bf16[512,256]{1,0:T(8,128)(2,1)S(1)}, bf16[512,256]{1,0:T(8,128)(2,1)S(1)}, u32[]{:S(2)}, u32[]{:S(2)}) %collective-permute-start.18) | collective-permute-done | bytes 262176 | tf_op jit(solution)/shard_map/ppermute | solution.py:640
  152.1 2.6 %collective-permute-start.21 = (bf16[512,256]{1,0:T(8,128)(2,1)S(1)}, bf16[512,256]{1,0:T(8,128)(2,1)S(1)}, u32[]{:S(2)}, u32[]{:S(2)}) collective-permute-start(bf16[512,256]{1,0:T(8,128)(2,1)S(1)} %add_convert_fusion.refs_0_), channel_id=1, source_target_pairs={{0,6},{1,7},{2,4},{3,5},{4,2},{5,3},{6,0},{7,1},{8,14},{9,15},{10,... | collective-permute-start | bytes 786440 | tf_op jit(solution)/shard_map/ppermute | solution.py:495
  155.7 7.9 %attend_backward.5 = bf16[2048,384]{1,0:T(8,128)(2,1)} custom-call(s32[16,10]{1,0:T(8,128)} %bitcast.26, s32[16]{0:T(128)} %bitcast.29, bf16[2048,768]{1,0:T(8,128)(2,1)} %bitcast.18, bf16[2048,256]{1,0:T(8,128)(2,1)} %copy-done.5, bf16[2048,128]{1,0:T(8,128)(2,1)} %copy-done.6, f32[2,128,256]{2,1,0:T(8,128)} %copy-done.8, ...), custom_call_target="tpu_custom_call" | custom-call | flops 3355443200 | bytes 786432 | tf_op jit(solution)/shard_map/attend_backward/pallas_call | solution.py:350
  163.6 2.7 %collective-permute-done.20.refs_4_ = bf16[512,256]{1,0:T(8,128)(2,1)S(1)} collective-permute-done((bf16[512,256]{1,0:T(8,128)(2,1)S(1)}, bf16[512,256]{1,0:T(8,128)(2,1)S(1)}, u32[]{:S(2)}, u32[]{:S(2)}) %collective-permute-start.20) | collective-permute-done | bytes 262176 | tf_op jit(solution)/shard_map/ppermute | solution.py:495
  167.0 3.6 %all-to-all-start.3 = ((bf16[8,256,384]{2,1,0:T(8,128)(2,1)}), bf16[8,256,384]{2,1,0:T(8,128)(2,1)S(1)}, u32[]{:S(2)}, u32[]{:S(2)}) async-start(bf16[8,256,384]{2,1,0:T(8,128)(2,1)} %bitcast.33), calls=%async_computation.3 | async-start | bytes 3145728 | tf_op jit(solution)/shard_map/all_to_all | solution.py:474
  173.8 3.4 %spread.1 = f32[512,2048]{1,0:T(8,128)} custom-call(bf16[512,256]{1,0:T(8,128)(2,1)} %copy-done.9, bf16[512,256]{1,0:T(8,128)(2,1)} %copy-done.12, bf16[512,256]{1,0:T(8,128)(2,1)} %collective-permute-done.19.refs_2_, bf16[512,256]{1,0:T(8,128)(2,1)} %copy-done.13, bf16[512,256]{1,0:T(8,128)(2,1)} %copy-done.11, ...), custom_call_target="tpu_custom_call" | custom-call | tf_op jit(solution)/shard_map/spread/pallas_call | solution.py:462
  177.3 14.3 %all-to-all-done.3.second = bf16[8,256,384]{2,1,0:T(8,128)(2,1)S(1)} async-done(((bf16[8,256,384]{2,1,0:T(8,128)(2,1)}), bf16[8,256,384]{2,1,0:T(8,128)(2,1)S(1)}, u32[]{:S(2)}, u32[]{:S(2)}) %all-to-all-start.3) | async-done | bytes 1572896 | tf_op jit(solution)/shard_map/all_to_all | solution.py:474
  191.6 2.4 %unpack.1 = (bf16[256,2048]{1,0:T(8,128)(2,1)}, bf16[256,2048]{1,0:T(8,128)(2,1)}, bf16[256,2048]{1,0:T(8,128)(2,1)}) custom-call(bf16[8,256,384]{2,1,0:T(8,128)(2,1)S(1)} %all-to-all-done.2.first, bf16[8,256,384]{2,1,0:T(8,128)(2,1)S(1)} %all-to-all-done.3.second), custom_call_target="tpu_custom_call" | custom-call | tf_op jit(solution)/shard_map/unpack/pallas_call | solution.py:439
  (79 shorter events, 18.8 us)
Async XLA Ops:
  5.2 41.8 %all-to-all-start = ((bf16[8,256,768]{2,1,0:T(8,128)(2,1)}), bf16[8,256,768]{2,1,0:T(8,128)(2,1)S(1)}, u32[]{:S(2)}, u32[]{:S(2)}) async-start(bf16[8,256,768]{2,1,0:T(8,128)(2,1)} %get-tuple-element.56), calls=%async_computation | async-start | bytes 6291456 | tf_op jit(solution)/shard_map/all_to_all | solution.py:474
  9.0 3.6 %collective-permute-start.1 = (bf16[256,2048]{1,0:T(8,128)(2,1)}, bf16[256,2048]{1,0:T(8,128)(2,1)}, u32[]{:S(2)}, u32[]{:S(2)}) collective-permute-start(bf16[256,2048]{1,0:T(8,128)(2,1)} %bitcast.20), channel_id=1, source_target_pairs={{0,1},{1,0},{2,3},{3,2},{4,5},{5,4},{6,7},{7,6},{8,9},{9,8},{10,11... | collective-permute-start | bytes 3145736 | tf_op jit(solution)/shard_map/ppermute | solution.py:495
  9.5 3.1 %collective-permute-start = (bf16[256,2048]{1,0:T(8,128)(2,1)}, bf16[256,2048]{1,0:T(8,128)(2,1)}, u32[]{:S(2)}, u32[]{:S(2)}) collective-permute-start(bf16[256,2048]{1,0:T(8,128)(2,1)} %get-tuple-element.59.refs_14_), channel_id=1, source_target_pairs={{0,8},{1,9},{10,18},{11,19},{20,12},{21,13},{30,22},{31,23}} | collective-permute-start | bytes 3145736 | tf_op jit(solution)/shard_map/ppermute | solution.py:490
  11.2 50.5 %collective-permute-start.2 = (bf16[256,2048]{1,0:T(8,128)(2,1)}, bf16[256,2048]{1,0:T(8,128)(2,1)}, u32[]{:S(2)}, u32[]{:S(2)}) collective-permute-start(bf16[256,2048]{1,0:T(8,128)(2,1)} %get-tuple-element.59.refs_14_), channel_id=1, source_target_pairs={{0,16},{1,17},{10,26},{11,27},{20,4},{21,5},{30,14},{31,15}} | collective-permute-start | bytes 3145736 | tf_op jit(solution)/shard_map/ppermute | solution.py:490
  46.9 28.2 %collective-permute-start.5 = (bf16[128,2048]{1,0:T(8,128)(2,1)}, bf16[128,2048]{1,0:T(8,128)(2,1)S(1)}, u32[]{:S(2)}, u32[]{:S(2)}) collective-permute-start(bf16[128,2048]{1,0:T(8,128)(2,1)} %get-tuple-element.72), channel_id=1, source_target_pairs={{0,4},{1,5},{2,6},{3,7},{4,0},{5,1},{6,2},{7,3},{8,12},{9,13},{10,... | collective-permute-start | bytes 1572872 | tf_op jit(solution)/shard_map/ppermute | solution.py:495
  47.5 27.6 %collective-permute-start.3 = (bf16[128,2048]{1,0:T(8,128)(2,1)}, bf16[128,2048]{1,0:T(8,128)(2,1)S(1)}, u32[]{:S(2)}, u32[]{:S(2)}) collective-permute-start(bf16[128,2048]{1,0:T(8,128)(2,1)} %get-tuple-element.72), channel_id=1, source_target_pairs={{0,2},{1,3},{2,0},{3,1},{4,6},{5,7},{6,4},{7,5},{8,10},{9,11},{10,... | collective-permute-start | bytes 1572872 | tf_op jit(solution)/shard_map/ppermute | solution.py:495
  48.1 27.0 %collective-permute-start.6 = (bf16[128,2048]{1,0:T(8,128)(2,1)}, bf16[128,2048]{1,0:T(8,128)(2,1)S(1)}, u32[]{:S(2)}, u32[]{:S(2)}) collective-permute-start(bf16[128,2048]{1,0:T(8,128)(2,1)} %get-tuple-element.73), channel_id=1, source_target_pairs={{0,4},{1,5},{2,6},{3,7},{4,0},{5,1},{6,2},{7,3},{8,12},{9,13},{10,... | collective-permute-start | bytes 1572872 | tf_op jit(solution)/shard_map/ppermute | solution.py:495
  49.4 25.7 %collective-permute-start.4 = (bf16[128,2048]{1,0:T(8,128)(2,1)}, bf16[128,2048]{1,0:T(8,128)(2,1)S(1)}, u32[]{:S(2)}, u32[]{:S(2)}) collective-permute-start(bf16[128,2048]{1,0:T(8,128)(2,1)} %get-tuple-element.73), channel_id=1, source_target_pairs={{0,2},{1,3},{2,0},{3,1},{4,6},{5,7},{6,4},{7,5},{8,10},{9,11},{10,... | collective-permute-start | bytes 1572872 | tf_op jit(solution)/shard_map/ppermute | solution.py:495
  63.0 27.2 %collective-permute-start.15 = (bf16[256,2048]{1,0:T(8,128)(2,1)S(1)}, bf16[256,2048]{1,0:T(8,128)(2,1)S(1)}, u32[]{:S(2)}, u32[]{:S(2)}) collective-permute-start(bf16[256,2048]{1,0:T(8,128)(2,1)S(1)} %broadcast_select_fusion), channel_id=1, source_target_pairs={{16,24},{17,25},{10,2},{11,3},{20,28},{21,29},{14,6},{15,7}} | collective-permute-start | bytes 3145736 | tf_op jit(solution)/shard_map/ppermute | solution.py:490
  75.2 2.6 %collective-permute-start.9 = (bf16[128,2048]{1,0:T(8,128)(2,1)S(1)}, bf16[128,2048]{1,0:T(8,128)(2,1)S(1)}, u32[]{:S(2)}, u32[]{:S(2)}) collective-permute-start(bf16[128,2048]{1,0:T(8,128)(2,1)S(1)} %collective-permute-done.5.refs_6_), channel_id=1, source_target_pairs={{0,1},{1,0},{2,3},{3,2},{4,5},{5,4},{6,7},{7,6},{8,9},{9,8},{10,11... | collective-permute-start | bytes 1572872 | tf_op jit(solution)/shard_map/ppermute | solution.py:495
  75.7 13.9 %collective-permute-start.11 = (bf16[128,2048]{1,0:T(8,128)(2,1)S(1)}, bf16[128,2048]{1,0:T(8,128)(2,1)S(1)}, u32[]{:S(2)}, u32[]{:S(2)}) collective-permute-start(bf16[128,2048]{1,0:T(8,128)(2,1)S(1)} %collective-permute-done.3.refs_2_), channel_id=1, source_target_pairs={{0,4},{1,5},{2,6},{3,7},{4,0},{5,1},{6,2},{7,3},{8,12},{9,13},{10,... | collective-permute-start | bytes 1572872 | tf_op jit(solution)/shard_map/ppermute | solution.py:495
  75.7 13.9 %collective-permute-start.13 = (bf16[128,2048]{1,0:T(8,128)(2,1)S(1)}, bf16[128,2048]{1,0:T(8,128)(2,1)S(1)}, u32[]{:S(2)}, u32[]{:S(2)}) collective-permute-start(bf16[128,2048]{1,0:T(8,128)(2,1)S(1)} %collective-permute-done.6.refs_8_), channel_id=1, source_target_pairs={{0,2},{1,3},{2,0},{3,1},{4,6},{5,7},{6,4},{7,5},{8,10},{9,11},{10,... | collective-permute-start | bytes 1572872 | tf_op jit(solution)/shard_map/ppermute | solution.py:495
  77.1 13.0 %collective-permute-start.7 = (bf16[128,2048]{1,0:T(8,128)(2,1)S(1)}, bf16[128,2048]{1,0:T(8,128)(2,1)S(1)}, u32[]{:S(2)}, u32[]{:S(2)}) collective-permute-start(bf16[128,2048]{1,0:T(8,128)(2,1)S(1)} %collective-permute-done.3.refs_2_), channel_id=1, source_target_pairs={{0,1},{1,0},{2,3},{3,2},{4,5},{5,4},{6,7},{7,6},{8,9},{9,8},{10,11... | collective-permute-start | bytes 1572872 | tf_op jit(solution)/shard_map/ppermute | solution.py:495
  77.9 12.3 %collective-permute-start.10 = (bf16[128,2048]{1,0:T(8,128)(2,1)S(1)}, bf16[128,2048]{1,0:T(8,128)(2,1)S(1)}, u32[]{:S(2)}, u32[]{:S(2)}) collective-permute-start(bf16[128,2048]{1,0:T(8,128)(2,1)S(1)} %collective-permute-done.6.refs_8_), channel_id=1, source_target_pairs={{0,1},{1,0},{2,3},{3,2},{4,5},{5,4},{6,7},{7,6},{8,9},{9,8},{10,11... | collective-permute-start | bytes 1572872 | tf_op jit(solution)/shard_map/ppermute | solution.py:495
  89.6 2.7 %collective-permute-start.14 = (bf16[128,2048]{1,0:T(8,128)(2,1)S(1)}, bf16[128,2048]{1,0:T(8,128)(2,1)S(1)}, u32[]{:S(2)}, u32[]{:S(2)}) collective-permute-start(bf16[128,2048]{1,0:T(8,128)(2,1)S(1)} %collective-permute-done.13.refs_12_), channel_id=1, source_target_pairs={{0,1},{1,0},{2,3},{3,2},{4,5},{5,4},{6,7},{7,6},{8,9},{9,8},{10,11... | collective-permute-start | bytes 1572872 | tf_op jit(solution)/shard_map/ppermute | solution.py:495
  100.6 20.3 %all-to-all-start.1 = ((bf16[8,256,256]{2,1,0:T(8,128)(2,1)}), bf16[8,256,256]{2,1,0:T(8,128)(2,1)S(1)}, u32[]{:S(2)}, u32[]{:S(2)}) async-start(bf16[8,256,256]{2,1,0:T(8,128)(2,1)} %get-tuple-element.84), calls=%async_computation.1 | async-start | bytes 2097152 | tf_op jit(solution)/shard_map/all_to_all | solution.py:474
  120.9 46.1 %all-to-all-start.2 = ((bf16[8,256,384]{2,1,0:T(8,128)(2,1)}), bf16[8,256,384]{2,1,0:T(8,128)(2,1)S(1)}, u32[]{:S(2)}, u32[]{:S(2)}) async-start(bf16[8,256,384]{2,1,0:T(8,128)(2,1)} %bitcast.32), calls=%async_computation.2 | async-start | bytes 3145728 | tf_op jit(solution)/shard_map/all_to_all | solution.py:474
  125.1 16.9 %collective-permute-start.16 = (bf16[512,256]{1,0:T(8,128)(2,1)S(1)}, bf16[512,256]{1,0:T(8,128)(2,1)S(1)}, u32[]{:S(2)}, u32[]{:S(2)}) collective-permute-start(bf16[512,256]{1,0:T(8,128)(2,1)S(1)} %get-tuple-element.90), channel_id=1, source_target_pairs={{0,8},{8,0},{16,24},{24,16},{1,9},{9,1},{17,25},{25,17},{2,10},{10... | collective-permute-start | bytes 786440 | tf_op jit(solution)/shard_map/ppermute | solution.py:640
  125.2 20.7 %collective-permute-start.17 = (bf16[512,256]{1,0:T(8,128)(2,1)S(1)}, bf16[512,256]{1,0:T(8,128)(2,1)S(1)}, u32[]{:S(2)}, u32[]{:S(2)}) collective-permute-start(bf16[512,256]{1,0:T(8,128)(2,1)S(1)} %get-tuple-element.91), channel_id=1, source_target_pairs={{0,16},{8,24},{16,0},{24,8},{1,17},{9,25},{17,1},{25,9},{2,18},{10... | collective-permute-start | bytes 786440 | tf_op jit(solution)/shard_map/ppermute | solution.py:640
  127.9 24.0 %collective-permute-start.18 = (bf16[512,256]{1,0:T(8,128)(2,1)S(1)}, bf16[512,256]{1,0:T(8,128)(2,1)S(1)}, u32[]{:S(2)}, u32[]{:S(2)}) collective-permute-start(bf16[512,256]{1,0:T(8,128)(2,1)S(1)} %get-tuple-element.92), channel_id=1, source_target_pairs={{0,24},{8,16},{16,8},{24,0},{1,25},{9,17},{17,9},{25,1},{2,26},{10... | collective-permute-start | bytes 786440 | tf_op jit(solution)/shard_map/ppermute | solution.py:640
  152.1 11.5 %collective-permute-start.21 = (bf16[512,256]{1,0:T(8,128)(2,1)S(1)}, bf16[512,256]{1,0:T(8,128)(2,1)S(1)}, u32[]{:S(2)}, u32[]{:S(2)}) collective-permute-start(bf16[512,256]{1,0:T(8,128)(2,1)S(1)} %add_convert_fusion.refs_0_), channel_id=1, source_target_pairs={{0,6},{1,7},{2,4},{3,5},{4,2},{5,3},{6,0},{7,1},{8,14},{9,15},{10,... | collective-permute-start | bytes 786440 | tf_op jit(solution)/shard_map/ppermute | solution.py:495
  154.8 11.6 %collective-permute-start.20 = (bf16[512,256]{1,0:T(8,128)(2,1)S(1)}, bf16[512,256]{1,0:T(8,128)(2,1)S(1)}, u32[]{:S(2)}, u32[]{:S(2)}) collective-permute-start(bf16[512,256]{1,0:T(8,128)(2,1)S(1)} %add_convert_fusion.refs_0_), channel_id=1, source_target_pairs={{0,4},{1,5},{2,6},{3,7},{4,0},{5,1},{6,2},{7,3},{8,12},{9,13},{10,... | collective-permute-start | bytes 786440 | tf_op jit(solution)/shard_map/ppermute | solution.py:495
  155.3 11.7 %collective-permute-start.19 = (bf16[512,256]{1,0:T(8,128)(2,1)S(1)}, bf16[512,256]{1,0:T(8,128)(2,1)}, u32[]{:S(2)}, u32[]{:S(2)}) collective-permute-start(bf16[512,256]{1,0:T(8,128)(2,1)S(1)} %add_convert_fusion.refs_0_), channel_id=1, source_target_pairs={{0,2},{1,3},{2,0},{3,1},{4,6},{5,7},{6,4},{7,5},{8,10},{9,11},{10,... | collective-permute-start | bytes 786440 | tf_op jit(solution)/shard_map/ppermute | solution.py:495
  167.0 24.5 %all-to-all-start.3 = ((bf16[8,256,384]{2,1,0:T(8,128)(2,1)}), bf16[8,256,384]{2,1,0:T(8,128)(2,1)S(1)}, u32[]{:S(2)}, u32[]{:S(2)}) async-start(bf16[8,256,384]{2,1,0:T(8,128)(2,1)} %bitcast.33), calls=%async_computation.3 | async-start | bytes 3145728 | tf_op jit(solution)/shard_map/all_to_all | solution.py:474
  (21 other events, 251.4 us)
